TPU v7x, 32 devices: a whole 2x2x4 slice. The times are simulated.
32 devices in a mesh: section: 4 (over y, x), dp: 8 (over z, core).
Axes of the slice: x: 2, y: 2, z: 4, core: 2. Of those that a mesh axis runs over, the one named last changes fastest.
Arguments:
- inputs: bfloat16 [2, 4096, 1024], P(None, 'dp'), may hold values from -6 to 6
- cotangent: bfloat16 [2, 4096, 1024], P(None, 'dp'), may hold values from -6 to 6
- seq_lengths: int32 [2, 8, 2], P(None, 'dp'), may hold values from 1 to 511, as said below
- flat_params: float32 [4, 8455168], P('section', 'dp'), may hold values from -8 to 8, as said below
Outputs:
- section_outputs: bfloat16 [4, 2, 4096, 1024], P('section', None, 'dp')
- section_grads: bfloat16 [4, 2, 4096, 1024], P('section', None, 'dp')
- param_grads: float32 [4, 8455168], P('section', 'dp')
- gain_grads: float32 [4, 1024], P('section')
Inputs may be any that keep to these rules, and one draw needn't show every extreme that they name: `seq_lengths`: each row's lengths sum to 512; its first sequence has 256 tokens or more. `flat_params`: entries after a sub-layer's own matrices are zero.
All inputs are finite; a program needn't handle non-finite values.
Results may differ from a plain program's by a relative error of at most 0.023.
Values may be sent and summed in bfloat16 or wider, within the bound.
No kernel may reach another device: no remote copies, remote signals or barrier semaphores. Data moves between devices by JAX's collectives and lax.ppermute only.
A program may use at most 832 MiB of HBM per device.

v0:
```python
from functools import partial

import jax
import jax.numpy as jnp
from jax import lax
from jax.sharding import PartitionSpec as P

D = 1024
FF = 2752
HEADS = 16
FEAT = 16
WINDOW = 64


EPS = 1e-05
NEG_LARGE = -1e30


def shortened(x):

    def short(part):
        return part.astype(jnp.bfloat16) if part.dtype == jnp.float32 else part

    return jax.tree.map(short, x)


def passed_along(value, axis, steps):
    count = lax.axis_size(axis)
    initial, last = (max(0, -steps), min(count, count - steps))
    return lax.ppermute(value, axis, [(source, source + steps) for source in range(initial, last)])


def layout(section_kind):
    if section_kind == 0:
        return [(1, D), (D, HEADS * FEAT), (D, HEADS * FEAT), (D, D), (D, D)]
    if section_kind == 2:
        return [(1, D), (D, D), (D, D), (D, D), (D, D)]
    return [(1, D), (D, FF), (D, FF), (FF, D)]


def unpack(flat_vec, section_kind):
    pieces = []
    offset = 0
    for row_count, col_count in layout(section_kind):
        pieces.append(
            flat_vec[offset : offset + row_count * col_count].reshape(row_count, col_count)
        )
        offset += row_count * col_count
    return pieces


def flatten_grads(grad_pieces, total_size):
    joined = jnp.concatenate([grad_piece.reshape(-1) for grad_piece in grad_pieces])
    return jnp.pad(joined, (0, total_size - joined.shape[0]))


def dot_plain(first_op, second_op):
    return jnp.dot(first_op, second_op, preferred_element_type=jnp.float32)


def dot_left(first_op, second_op):
    return lax.dot_general(
        first_op, second_op, (((0,), (0,)), ((), ())), preferred_element_type=jnp.float32
    )


def dot_right(first_op, second_op):
    return lax.dot_general(
        first_op, second_op, (((1,), (1,)), ((), ())), preferred_element_type=jnp.float32
    )


def segment_ids(lengths_row, total_rows):
    doc_ends = jnp.cumsum(lengths_row)
    positions = jnp.arange(total_rows, dtype=jnp.int32)
    return jnp.sum((positions[:, None] >= doc_ends[None, :]).astype(jnp.int32), axis=1)


def norm_forward(entry_val, gain_f32):
    inv_root = lax.rsqrt(jnp.mean(entry_val * entry_val, axis=-1, keepdims=True) + EPS)
    normed = entry_val * inv_root
    return (normed * gain_f32, normed, inv_root)


def norm_backward(grad_hidden, gain_f32, normed, inv_root):
    grad_normed = grad_hidden * gain_f32
    grad_gain = jnp.sum(grad_hidden * normed, axis=0, keepdims=True)
    grad_entry = inv_root * (
        grad_normed - normed * jnp.mean(grad_normed * normed, axis=-1, keepdims=True)
    )
    return (grad_entry, grad_gain)


def block_weights(section_kind, query_rows, key_row_block, seg_ids, start_row_index, block_size):
    final_row_index = start_row_index + block_size
    first_key = 0 if section_kind == 0 else max(0, start_row_index - WINDOW)
    score_scaling_factor = 0.25 if section_kind == 0 else 0.125
    score_matrix = (
        jnp.einsum(
            "ezl,jzl->zej",
            query_rows[start_row_index:final_row_index],
            key_row_block[first_key:final_row_index],
            preferred_element_type=jnp.float32,
        )
        * score_scaling_factor
    )
    query_pos = start_row_index + jnp.arange(block_size, dtype=jnp.int32)
    key_pos = first_key + jnp.arange(final_row_index - first_key, dtype=jnp.int32)
    allowed = (key_pos[None, :] <= query_pos[:, None]) & (
        seg_ids[first_key:final_row_index][None, :]
        == seg_ids[start_row_index:final_row_index][:, None]
    )
    if section_kind == 0:
        weights = jnp.where(
            allowed[None], 1.0 + score_matrix + 0.5 * score_matrix * score_matrix, 0.0
        )
        totals = jnp.sum(weights, axis=-1, keepdims=True)
        return (score_matrix, allowed, weights / totals, totals, first_key)
    allowed = allowed & (query_pos[:, None] - key_pos[None, :] < WINDOW)
    masked = jnp.where(allowed[None], score_matrix, NEG_LARGE)
    exponent = jnp.where(
        allowed[None], jnp.exp(masked - jnp.max(masked, axis=-1, keepdims=True)), 0.0
    )
    totals = jnp.sum(exponent, axis=-1, keepdims=True)
    return (score_matrix, allowed, exponent / totals, totals, first_key)


def mix_forward(section_kind, query_rows, key_row_block, values, seg_ids):
    row_total = query_rows.shape[0]
    block_size = min(512, row_total)
    outputs = []
    for start_row_index in range(0, row_total, block_size):
        score_matrix, allowed, soft_weights, totals, first_key = block_weights(
            section_kind, query_rows, key_row_block, seg_ids, start_row_index, block_size
        )
        outputs.append(
            jnp.einsum(
                "hqk,khv->qhv",
                soft_weights.astype(jnp.bfloat16),
                values[first_key : start_row_index + block_size],
                preferred_element_type=jnp.float32,
            )
        )
    return jnp.concatenate(outputs, axis=0).astype(jnp.bfloat16)


def mix_backward(section_kind, query_rows, key_row_block, values, seg_ids, grad_mixed):
    row_total = query_rows.shape[0]
    block_size = min(512, row_total)
    score_scaling_factor = 0.25 if section_kind == 0 else 0.125
    grad_query_parts = []
    mixed_parts = []
    grad_keys = jnp.zeros(key_row_block.shape, jnp.float32)
    grad_values = jnp.zeros(values.shape, jnp.float32)
    for start_row_index in range(0, row_total, block_size):
        final_row_index = start_row_index + block_size
        score_matrix, allowed, soft_weights, totals, first_key = block_weights(
            section_kind, query_rows, key_row_block, seg_ids, start_row_index, block_size
        )
        rounded_weights = soft_weights.astype(jnp.bfloat16)
        value_block = values[first_key:final_row_index]
        grad_block = grad_mixed[start_row_index:final_row_index]
        mixed_parts.append(
            jnp.einsum(
                "hqk,khv->qhv", rounded_weights, value_block, preferred_element_type=jnp.float32
            )
        )
        grad_values = grad_values.at[first_key:final_row_index].add(
            jnp.einsum(
                "hqk,qhv->khv", rounded_weights, grad_block, preferred_element_type=jnp.float32
            )
        )
        grad_weights = jnp.einsum(
            "qhv,khv->hqk", grad_block, value_block, preferred_element_type=jnp.float32
        )
        centred = grad_weights - jnp.sum(grad_weights * soft_weights, axis=-1, keepdims=True)
        if section_kind == 0:
            grad_scores = jnp.where(allowed[None], centred * (1.0 + score_matrix) / totals, 0.0)
        else:
            grad_scores = jnp.where(allowed[None], soft_weights * centred, 0.0)
        grad_scores = grad_scores.astype(jnp.bfloat16)
        grad_query_parts.append(
            jnp.einsum(
                "ncw,wne->cne",
                grad_scores,
                key_row_block[first_key:final_row_index],
                preferred_element_type=jnp.float32,
            )
            * score_scaling_factor
        )
        grad_keys = grad_keys.at[first_key:final_row_index].add(
            jnp.einsum(
                "zas,aze->sze",
                grad_scores,
                query_rows[start_row_index:final_row_index],
                preferred_element_type=jnp.float32,
            )
            * score_scaling_factor
        )
    mixed_out = jnp.concatenate(mixed_parts, axis=0).astype(jnp.bfloat16)
    grad_query = jnp.concatenate(grad_query_parts, axis=0).astype(jnp.bfloat16)
    return (mixed_out, grad_query, grad_keys.astype(jnp.bfloat16), grad_values.astype(jnp.bfloat16))


def attention_setup(flat_vec, residual, section_kind):
    norm_gain, w_query, w_key, w_value, w_out = unpack(flat_vec, section_kind)
    entry_val = residual.astype(jnp.float32)
    gain_f32 = norm_gain.astype(jnp.float32)
    normed_out, normed, inv_root = norm_forward(entry_val, gain_f32)
    hidden = normed_out.astype(jnp.bfloat16)
    row_total = residual.shape[0]
    query_rows = dot_plain(hidden, w_query).astype(jnp.bfloat16).reshape(row_total, HEADS, -1)
    key_row_block = dot_plain(hidden, w_key).astype(jnp.bfloat16).reshape(row_total, HEADS, -1)
    values = dot_plain(hidden, w_value).astype(jnp.bfloat16).reshape(row_total, HEADS, -1)
    return (
        w_query,
        w_key,
        w_value,
        w_out,
        entry_val,
        gain_f32,
        normed,
        inv_root,
        hidden,
        query_rows,
        key_row_block,
        values,
    )


def attention_forward(flat_vec, residual, seg_ids, section_kind):
    (
        w_query,
        w_key,
        w_value,
        w_out,
        entry_val,
        gain_f32,
        normed,
        inv_root,
        hidden,
        query_rows,
        key_row_block,
        values,
    ) = attention_setup(flat_vec, residual, section_kind)
    mixed_out = mix_forward(section_kind, query_rows, key_row_block, values, seg_ids)
    branch_out = dot_plain(mixed_out.reshape(residual.shape[0], -1), w_out)
    return (entry_val + branch_out).astype(jnp.bfloat16)


def attention_backward(flat_vec, residual, seg_ids, grad_out, section_kind):
    (
        w_query,
        w_key,
        w_value,
        w_out,
        entry_val,
        gain_f32,
        normed,
        inv_root,
        hidden,
        query_rows,
        key_row_block,
        values,
    ) = attention_setup(flat_vec, residual, section_kind)
    row_total = residual.shape[0]
    grad_mixed = dot_right(grad_out, w_out).astype(jnp.bfloat16).reshape(row_total, HEADS, -1)
    mixed_out, grad_query, grad_keys, grad_values = mix_backward(
        section_kind, query_rows, key_row_block, values, seg_ids, grad_mixed
    )
    grad_w_out = dot_left(mixed_out.reshape(row_total, -1), grad_out)
    grad_query = grad_query.reshape(row_total, -1)
    grad_keys = grad_keys.reshape(row_total, -1)
    grad_values = grad_values.reshape(row_total, -1)
    grad_hidden = (
        dot_right(grad_query, w_query)
        + dot_right(grad_keys, w_key)
        + dot_right(grad_values, w_value)
    )
    grad_entry, grad_gain = norm_backward(grad_hidden, gain_f32, normed, inv_root)
    grad_in = (grad_out.astype(jnp.float32) + grad_entry).astype(jnp.bfloat16)
    grad_flat = flatten_grads(
        [
            grad_gain,
            dot_left(hidden, grad_query),
            dot_left(hidden, grad_keys),
            dot_left(hidden, grad_values),
            grad_w_out,
        ],
        flat_vec.shape[0],
    )
    return (grad_in, grad_flat)


def mlp_setup(flat_vec, residual):
    norm_gain, w_gate, w_up, w_down = unpack(flat_vec, 1)
    entry_val = residual.astype(jnp.float32)
    gain_f32 = norm_gain.astype(jnp.float32)
    normed_out, normed, inv_root = norm_forward(entry_val, gain_f32)
    hidden = normed_out.astype(jnp.bfloat16)
    gate_pre = dot_plain(hidden, w_gate)
    up_pre = dot_plain(hidden, w_up)
    return (w_gate, w_up, w_down, entry_val, gain_f32, normed, inv_root, hidden, gate_pre, up_pre)


def mlp_forward(flat_vec, residual, seg_ids):
    w_gate, w_up, w_down, entry_val, gain_f32, normed, inv_root, hidden, gate_pre, up_pre = (
        mlp_setup(flat_vec, residual)
    )
    activation = (jax.nn.silu(gate_pre) * up_pre).astype(jnp.bfloat16)
    return (entry_val + dot_plain(activation, w_down)).astype(jnp.bfloat16)


def mlp_backward(flat_vec, residual, seg_ids, grad_out):
    w_gate, w_up, w_down, entry_val, gain_f32, normed, inv_root, hidden, gate_pre, up_pre = (
        mlp_setup(flat_vec, residual)
    )
    sigmoid_gate = jax.nn.sigmoid(gate_pre)
    silu_gate = gate_pre * sigmoid_gate
    activation = (silu_gate * up_pre).astype(jnp.bfloat16)
    grad_w_down = dot_left(activation, grad_out)
    grad_activation = dot_right(grad_out, w_down)
    grad_gate = (
        grad_activation * up_pre * sigmoid_gate * (1.0 + gate_pre * (1.0 - sigmoid_gate))
    ).astype(jnp.bfloat16)
    grad_up = (grad_activation * silu_gate).astype(jnp.bfloat16)
    grad_hidden = dot_right(grad_gate, w_gate) + dot_right(grad_up, w_up)
    grad_entry, grad_gain = norm_backward(grad_hidden, gain_f32, normed, inv_root)
    grad_in = (grad_out.astype(jnp.float32) + grad_entry).astype(jnp.bfloat16)
    grad_flat = flatten_grads(
        [grad_gain, dot_left(hidden, grad_gate), dot_left(hidden, grad_up), grad_w_down],
        flat_vec.shape[0],
    )
    return (grad_in, grad_flat)


def spare_forward(flat_vec, residual, seg_ids):
    return jnp.zeros_like(residual)


def spare_backward(flat_vec, residual, seg_ids, grad_out):
    return (jnp.zeros_like(residual), jnp.zeros(flat_vec.shape, jnp.float32))


def store_slot(buffer, new_value, slot_index, active):
    current = lax.dynamic_index_in_dim(buffer, slot_index, 0, keepdims=False)
    return lax.dynamic_update_slice_in_dim(
        buffer, jnp.where(active, new_value, current)[None], slot_index, 0
    )


def per_device(inputs, cotangent, seq_lengths, flat_params):
    section_now = lax.axis_index("section")
    section_count = lax.axis_size("section")
    micro_count = inputs.shape[0]
    row_total = inputs.shape[1]
    shard_low = flat_params.astype(jnp.bfloat16)
    gathered = lax.all_gather(shard_low, "dp", axis=1, tiled=True)[0]
    forward_fns = [
        partial(attention_forward, section_kind=0),
        mlp_forward,
        partial(attention_forward, section_kind=2),
        mlp_forward,
        spare_forward,
    ]
    backward_fns = [
        partial(attention_backward, section_kind=0),
        mlp_backward,
        partial(attention_backward, section_kind=2),
        mlp_backward,
        spare_backward,
    ]
    saved_inputs = jnp.zeros_like(inputs)
    produced = jnp.zeros_like(inputs)
    previous = jnp.zeros(inputs.shape[1:], jnp.bfloat16)
    for tick_step in range(micro_count + section_count - 1):
        micro_index = tick_step - section_now
        active = (micro_index >= 0) & (micro_index < micro_count)
        chosen = jnp.clip(micro_index, 0, micro_count - 1)
        if tick_step > 0:
            arrived = jax.tree.map(
                lambda part, own: part.astype(own.dtype),
                passed_along(shortened(previous), "section", 1),
                previous,
            )
        else:
            arrived = previous
        residual = jnp.where(
            section_now == 0, lax.dynamic_index_in_dim(inputs, chosen, 0, keepdims=False), arrived
        )
        lengths_row = lax.dynamic_index_in_dim(seq_lengths, chosen, 0, keepdims=False)[0]
        seg_ids = segment_ids(lengths_row, row_total)
        branch_index = jnp.where(active, section_now, 4)
        result = lax.switch(branch_index, forward_fns, gathered, residual, seg_ids)
        saved_inputs = store_slot(saved_inputs, residual, chosen, active)
        produced = store_slot(produced, result, chosen, active)
        previous = result
    back_weights = lax.all_gather(shard_low, "dp", axis=1, tiled=True)[0]
    grads_in = jnp.zeros_like(inputs)
    grad_total = jnp.zeros(gathered.shape, jnp.float32)
    gain_total = jnp.zeros((D,), jnp.float32)
    previous_grad = jnp.zeros(inputs.shape[1:], jnp.bfloat16)
    for tick_step in range(micro_count + section_count - 1):
        micro_index = micro_count - 1 - tick_step + (section_count - 1 - section_now)
        active = (micro_index >= 0) & (micro_index < micro_count)
        chosen = jnp.clip(micro_index, 0, micro_count - 1)
        if tick_step > 0:
            arrived = jax.tree.map(
                lambda part, own: part.astype(own.dtype),
                passed_along(shortened(previous_grad), "section", -1),
                previous_grad,
            )
        else:
            arrived = previous_grad
        grad_out = jnp.where(
            section_now == section_count - 1,
            lax.dynamic_index_in_dim(cotangent, chosen, 0, keepdims=False),
            arrived,
        )
        residual = lax.dynamic_index_in_dim(saved_inputs, chosen, 0, keepdims=False)
        lengths_row = lax.dynamic_index_in_dim(seq_lengths, chosen, 0, keepdims=False)[0]
        seg_ids = segment_ids(lengths_row, row_total)
        branch_index = jnp.where(active, section_now, 4)
        grad_in, grad_flat = lax.switch(
            branch_index, backward_fns, back_weights, residual, seg_ids, grad_out
        )
        grads_in = store_slot(grads_in, grad_in, chosen, active)
        gain_total = gain_total + grad_flat[0:D]
        grad_total = grad_total + grad_flat
        previous_grad = grad_in
    shard_total = lax.psum_scatter(grad_total[None], "dp", scatter_dimension=1, tiled=True)
    gain_grads = lax.psum(gain_total, "dp")[None]
    return (produced[None], grads_in[None], shard_total, gain_grads)


def solution(mesh):
    return jax.shard_map(
        per_device,
        mesh=mesh,
        in_specs=(
            P(None, "dp", None),
            P(None, "dp", None),
            P(None, "dp", None),
            P("section", "dp"),
        ),
        out_specs=(
            P("section", None, "dp", None),
            P("section", None, "dp", None),
            P("section", "dp"),
            P("section", None),
        ),
        check_vma=False,
    )
```

profile of v0, /device:TPU:0, one launch (start us, length us, event | category | flops | bytes accessed | tf_op | source)
XLA Modules:
  0.0 2940.5 jit_solution(10037551852204508429)
XLA Ops:
  17.0 290.8 %all-gather.2.cloned.1.call-done = bf16[1,8455168]{1,0:T(2,128)(2,1)} async-done(((bf16[1,1056896]{1,0:T(2,128)(2,1)}), bf16[1,8455168]{1,0:T(2,128)(2,1)}) %all-gather.2.cloned.1.call-update) | async-done | bytes 16910352 | tf_op jit(solution)/shard_map/all_gather | solution.py:358
  307.8 357.8 %reduce.40 = bf16[8455168]{0:T(1024)(128)(2,1)} reduce(bf16[1,8455168]{1,0:T(2,128)(2,1)} %all-gather.2.cloned.1.call-done, bf16[]{:T(256)} %constant.1360), dimensions={0}, to_apply=%all_gather.4.reduce_sub_computation | reduce | bytes 33820672 | tf_op jit(solution)/shard_map/all_gather | solution.py:358
  665.6 85.6 %conditional.10 = (bf16[512,1024]{1,0:T(8,128)(2,1)}) conditional(s32[]{:T(128)} %clamp.20, (bf16[512,1024]{1,0:T(8,128)(2,1)S(1)}, bf16[8455168]{0:T(1024)(128)(2,1)}, s32[512]{0:T(512)S(1)}) %tuple.323, (bf16[512,1024]{1,0:T(8,128)(2,1)S(1)}, bf16[8455168]{0:T(1024)(128)(2,1)}) %tuple.324, ...), branch_computations={%region_2.5_spmd, %region_5.7_spmd, %region_7.11_spmd, %region_11.... | conditional | flops 8672839680 | bytes 105480224 | solution.py:394
  708.8 14.2 fusion.6
  755.6 20.3 collective-permute-done
  777.6 79.4 %conditional.11 = (bf16[512,1024]{1,0:T(8,128)(2,1)}) conditional(s32[]{:T(128)} %clamp.21, (bf16[512,1024]{1,0:T(8,128)(2,1)S(1)}, bf16[8455168]{0:T(1024)(128)(2,1)}, s32[512]{0:T(512)}) %tuple.326, (bf16[512,1024]{1,0:T(8,128)(2,1)S(1)}, bf16[8455168]{0:T(1024)(128)(2,1)}) %tuple.327, ...), branch_computations={%region_16.19_spmd, %region_19.21_spmd, %region_21.25_spmd, %regio... | conditional | flops 8672839680 | bytes 113868896 | solution.py:394
  813.1 14.4 fusion.64
  876.4 16.2 collective-permute-done.1
  894.4 23.9 conditional.12
  918.3 66.0 %collective-permute-start.2 = (bf16[512,1024]{1,0:T(8,128)(2,1)}, bf16[512,1024]{1,0:T(8,128)(2,1)}, u32[]{:S(2)}, u32[]{:S(2)}) collective-permute-start(bf16[512,1024]{1,0:T(8,128)(2,1)} %get-tuple-element.1138), channel_id=1, source_target_pairs={{0,8},{8,16},{16,24},{1,9},{9,17},{17,25},{2,10},{10,18},{18,26},{... | collective-permute-start | bytes 3145736 | tf_op jit(solution)/shard_map/ppermute | solution.py:30
  986.4 18.7 collective-permute-done.2
  1006.8 25.0 conditional.13
  1041.5 17.0 collective-permute-done.3
  1065.7 50.2 %conditional.15 = (bf16[512,1024]{1,0:T(8,128)(2,1)}, f32[8455168]{0:T(1024)}) conditional(s32[]{:T(128)} %clamp.24, (bf16[512,1024]{1,0:T(8,128)(2,1)S(1)}, bf16[512,1024]{1,0:T(8,128)(2,1)S(1)}, bf16[8455168]{0:T(1024)(128)(2,1)}, s32[512]{0:T(512)S(1)}) %tuple.338, (bf16[512,1024]{1,0:T(8,128)(2,1)S(1)}, ...), branch_computations={%region_70.76_spmd, %region_76.80_spmd, %region_80.87_spmd, %regio... | conditional | flops 23156461568 | bytes 432214336 | solution.py:424
  1117.2 77.0 %collective-permute-done.4 = bf16[512,1024]{1,0:T(8,128)(2,1)S(1)} collective-permute-done((bf16[512,1024]{1,0:T(8,128)(2,1)}, bf16[512,1024]{1,0:T(8,128)(2,1)S(1)}, u32[]{:S(2)}, u32[]{:S(2)}) %collective-permute-start.4) | collective-permute-done | bytes 1048608 | tf_op jit(solution)/shard_map/ppermute | solution.py:30
  1195.6 38.5 %conditional.16 = (bf16[512,1024]{1,0:T(8,128)(2,1)}, f32[8455168]{0:T(1024)}) conditional(s32[]{:T(128)} %clamp.23, (bf16[512,1024]{1,0:T(8,128)(2,1)S(1)}, bf16[512,1024]{1,0:T(8,128)(2,1)S(1)}, bf16[8455168]{0:T(1024)(128)(2,1)}, s32[512]{0:T(512)}) %tuple.589, (bf16[512,1024]{1,0:T(8,128)(2,1)S(1)}, ...), branch_computations={%region_92.98_spmd, %region_98.102_spmd, %region_102.109_spmd, %re... | conditional | flops 23156461568 | bytes 432214336 | solution.py:424
  1235.4 24.0 collective-permute-done.5
  1260.8 50.2 %conditional.17 = (bf16[512,1024]{1,0:T(8,128)(2,1)}, f32[8455168]{0:T(1024)}) conditional(s32[]{:T(128)} %clamp.22, (bf16[512,1024]{1,0:T(8,128)(2,1)S(1)}, bf16[512,1024]{1,0:T(8,128)(2,1)S(1)}, bf16[8455168]{0:T(1024)(128)(2,1)}, s32[512]{0:T(512)S(1)}) %tuple.601, (bf16[512,1024]{1,0:T(8,128)(2,1)S(1)}, ...), branch_computations={%region_114.120_spmd, %region_120.124_spmd, %region_124.131_spmd, ... | conditional | flops 23156461568 | bytes 432214336 | solution.py:424
  1312.3 511.7 %collective-permute-done.6 = bf16[512,1024]{1,0:T(8,128)(2,1)S(1)} collective-permute-done((bf16[512,1024]{1,0:T(8,128)(2,1)}, bf16[512,1024]{1,0:T(8,128)(2,1)S(1)}, u32[]{:S(2)}, u32[]{:S(2)}) %collective-permute-start.6) | collective-permute-done | bytes 1048608 | tf_op jit(solution)/shard_map/ppermute | solution.py:30
  1825.5 161.2 %conditional.18 = (bf16[512,1024]{1,0:T(8,128)(2,1)}, f32[8455168]{0:T(1024)}) conditional(s32[]{:T(128)} %clamp.21, (bf16[512,1024]{1,0:T(8,128)(2,1)S(1)}, bf16[512,1024]{1,0:T(8,128)(2,1)S(1)}, bf16[8455168]{0:T(1024)(128)(2,1)}, s32[512]{0:T(512)}) %tuple.581, (bf16[512,1024]{1,0:T(8,128)(2,1)S(1)}, ...), branch_computations={%region_136.142_spmd, %region_142.146_spmd, %region_146.153_spmd, ... | conditional | flops 23156461568 | bytes 432214336 | solution.py:424
  1872.9 20.9 fusion.773
  1893.9 21.5 fusion.774
  1945.9 15.3 pad.88
  1988.0 67.7 %collective-permute-done.7 = bf16[512,1024]{1,0:T(8,128)(2,1)S(1)} collective-permute-done((bf16[512,1024]{1,0:T(8,128)(2,1)}, bf16[512,1024]{1,0:T(8,128)(2,1)S(1)}, u32[]{:S(2)}, u32[]{:S(2)}) %collective-permute-start.7) | collective-permute-done | bytes 1048608 | tf_op jit(solution)/shard_map/ppermute | solution.py:30
  2057.1 156.0 %conditional.19 = (bf16[512,1024]{1,0:T(8,128)(2,1)S(1)}, f32[8455168]{0:T(1024)}) conditional(s32[]{:T(128)} %clamp.20, (bf16[512,1024]{1,0:T(8,128)(2,1)S(1)}, bf16[512,1024]{1,0:T(8,128)(2,1)S(1)}, bf16[8455168]{0:T(1024)(128)(2,1)}, s32[512]{0:T(512)S(1)}) %tuple.597, (bf16[512,1024]{1,0:T(8,128)(2,1)S(1)}, ...), branch_computations={%region_158.164_spmd, %region_164.168_spmd, %region_168.175_spmd, ... | conditional | flops 23156461568 | bytes 432214336 | solution.py:424
  2098.8 20.9 fusion.924
  2119.7 21.6 fusion.925
  2170.7 15.3 pad.90
  2213.1 63.2 %add_add_fusion.10 = f32[8455168]{0:T(1024)} fusion(f32[8455168]{0:T(1024)} %get-tuple-element.813, f32[8455168]{0:T(1024)} %get-tuple-element.812, f32[8455168]{0:T(1024)} %get-tuple-element.811, f32[8455168]{0:T(1024)} %get-tuple-element.809, f32[8455168]{0:T(1024)} %get-tuple-element.810), kind=kLoop, calls=%fused_computation.1260 | loop fusion | flops 33820672 | bytes 202924032 | tf_op jit(solution)/shard_map/add | solution.py:429
  2281.9 19.3 conditional.14
  2308.8 15.0 psum.7
  2325.2 603.5 %all-reduce.13.cloned.1.call-done = f32[1,8455168]{1,0:T(1,128)} async-done(((f32[1,8455168]{1,0:T(1,128)}), f32[1,8455168]{1,0:T(1,128)}) %all-reduce.13.cloned.1.call-update) | async-done | bytes 33820688
  (280 shorter events, 361.2 us)
Async XLA Ops:
  7.2 300.6 %all-gather.2.cloned.1.call-start = ((), (), s32[]{:S(2)}) async-start(), calls=%async_computation | async-start | bytes 38048256 | tf_op jit(solution)/shard_map/all_gather | solution.py:358
  12.5 2916.2 %all-reduce.13.cloned.1.call-start = ((), (), s32[]{:S(2)}) async-start(), calls=%async_computation.1 | async-start | bytes 67641344
  14.0 651.6 %copy-start.102 = (s32[512]{0:T(512)}, s32[512]{0:T(512)S(1)}, u32[]{:S(2)}) copy-start(s32[512]{0:T(512)S(1)} %fusion.1046) | copy-start | bytes 6148
  665.6 87.9 %copy-start.114 = (s32[2,1]{0,1:T(1,128)S(1)}, s32[2,1]{0,1:T(1,128)}, u32[]{:S(2)}) copy-start(s32[2,1]{0,1:T(1,128)} %get-tuple-element.1081) | copy-start | bytes 28
  665.6 110.3 %copy-start.10 = (bf16[2,512,1024]{2,1,0:T(8,128)(2,1)S(1)}, bf16[2,512,1024]{2,1,0:T(8,128)(2,1)}, u32[]{:S(2)}) copy-start(bf16[2,512,1024]{2,1,0:T(8,128)(2,1)} %param.134) | copy-start | bytes 6291460
  751.2 24.7 collective-permute-start
  777.6 92.4 %copy-start.113 = (s32[2,1]{0,1:T(1,128)S(1)}, s32[2,1]{0,1:T(1,128)}, u32[]{:S(2)}) copy-start(s32[2,1]{0,1:T(1,128)} %get-tuple-element.1080) | copy-start | bytes 28
  857.0 15.2 copy-start.79
  857.0 35.6 %collective-permute-start.1 = (bf16[512,1024]{1,0:T(8,128)(2,1)}, bf16[512,1024]{1,0:T(8,128)(2,1)S(1)}, u32[]{:S(2)}, u32[]{:S(2)}) collective-permute-start(bf16[512,1024]{1,0:T(8,128)(2,1)} %get-tuple-element.1137), channel_id=1, source_target_pairs={{0,8},{8,16},{16,24},{1,9},{9,17},{17,25},{2,10},{10,18},{18,26},{... | collective-permute-start | bytes 3145736 | tf_op jit(solution)/shard_map/ppermute | solution.py:30
  870.3 24.0 copy-start.108
  872.2 20.4 copy-start.11
  894.4 89.9 %copy-start.112 = (s32[2,1]{0,1:T(1,128)S(1)}, s32[2,1]{0,1:T(1,128)}, u32[]{:S(2)}) copy-start(s32[2,1]{0,1:T(1,128)} %get-tuple-element.1083) | copy-start | bytes 28
  894.4 110.7 %copy-start.12 = (bf16[2,512,1024]{2,1,0:T(8,128)(2,1)S(1)}, bf16[2,512,1024]{2,1,0:T(8,128)(2,1)}, u32[]{:S(2)}) copy-start(bf16[2,512,1024]{2,1,0:T(8,128)(2,1)} %param.134) | copy-start | bytes 6291460
  918.3 86.7 %collective-permute-start.2 = (bf16[512,1024]{1,0:T(8,128)(2,1)}, bf16[512,1024]{1,0:T(8,128)(2,1)}, u32[]{:S(2)}, u32[]{:S(2)}) collective-permute-start(bf16[512,1024]{1,0:T(8,128)(2,1)} %get-tuple-element.1138), channel_id=1, source_target_pairs={{0,8},{8,16},{16,24},{1,9},{9,17},{17,25},{2,10},{10,18},{18,26},{... | collective-permute-start | bytes 3145736 | tf_op jit(solution)/shard_map/ppermute | solution.py:30
  1006.8 31.8 %copy-start.111 = (s32[2,1]{0,1:T(1,128)S(1)}, s32[2,1]{0,1:T(1,128)}, u32[]{:S(2)}) copy-start(s32[2,1]{0,1:T(1,128)} %get-tuple-element.1079) | copy-start | bytes 28
  1031.8 26.6 copy-start.13
  1031.9 26.6 collective-permute-start.3
  1038.9 26.8 copy-start.104
  1065.7 129.9 %copy-start.3 = (bf16[512,1024]{1,0:T(8,128)(2,1)S(1)}, bf16[512,1024]{1,0:T(8,128)(2,1)}, u32[]{:S(2)}) copy-start(bf16[512,1024]{1,0:T(8,128)(2,1)} %get-tuple-element.1075) | copy-start | bytes 3145732
  1115.9 78.3 %collective-permute-start.4 = (bf16[512,1024]{1,0:T(8,128)(2,1)}, bf16[512,1024]{1,0:T(8,128)(2,1)S(1)}, u32[]{:S(2)}, u32[]{:S(2)}) collective-permute-start(bf16[512,1024]{1,0:T(8,128)(2,1)} %get-tuple-element.804), channel_id=1, source_target_pairs={{8,0},{16,8},{24,16},{9,1},{17,9},{25,17},{10,2},{18,10},{26,18},{... | collective-permute-start | bytes 3145736 | tf_op jit(solution)/shard_map/ppermute | solution.py:30
  1195.6 65.2 %copy-start.2 = (bf16[512,1024]{1,0:T(8,128)(2,1)S(1)}, bf16[512,1024]{1,0:T(8,128)(2,1)}, u32[]{:S(2)}) copy-start(bf16[512,1024]{1,0:T(8,128)(2,1)} %get-tuple-element.1074) | copy-start | bytes 3145732
  1195.6 65.2 %copy-start.109 = (s32[512]{0:T(512)S(1)}, s32[512]{0:T(512)}, u32[]{:S(2)}) copy-start(s32[512]{0:T(512)} %copy-done.108) | copy-start | bytes 6148
  1234.1 25.3 collective-permute-start.5
  1260.8 564.6 %copy-start.1 = (bf16[512,1024]{1,0:T(8,128)(2,1)S(1)}, bf16[512,1024]{1,0:T(8,128)(2,1)}, u32[]{:S(2)}) copy-start(bf16[512,1024]{1,0:T(8,128)(2,1)} %get-tuple-element.1073) | copy-start | bytes 3145732
  1311.0 513.0 %collective-permute-start.6 = (bf16[512,1024]{1,0:T(8,128)(2,1)}, bf16[512,1024]{1,0:T(8,128)(2,1)S(1)}, u32[]{:S(2)}, u32[]{:S(2)}) collective-permute-start(bf16[512,1024]{1,0:T(8,128)(2,1)} %get-tuple-element.806), channel_id=1, source_target_pairs={{8,0},{16,8},{24,16},{9,1},{17,9},{25,17},{10,2},{18,10},{26,18},{... | collective-permute-start | bytes 3145736 | tf_op jit(solution)/shard_map/ppermute | solution.py:30
  1825.4 231.6 %copy-start = (bf16[512,1024]{1,0:T(8,128)(2,1)S(1)}, bf16[512,1024]{1,0:T(8,128)(2,1)}, u32[]{:S(2)}) copy-start(bf16[512,1024]{1,0:T(8,128)(2,1)} %get-tuple-element.1072) | copy-start | bytes 3145732
  1825.5 231.6 %copy-start.103 = (s32[512]{0:T(512)S(1)}, s32[512]{0:T(512)}, u32[]{:S(2)}) copy-start(s32[512]{0:T(512)} %copy-done.102) | copy-start | bytes 6148
  1827.4 45.5 %copy-start.93 = (pred[512,512]{0,1:T(8,128)(4,1)}, pred[512,512]{0,1:T(8,128)(4,1)S(1)}, u32[]{:S(2)}) copy-start(pred[512,512]{0,1:T(8,128)(4,1)S(1)} %fusion.775) | copy-start | bytes 786436 | tf_op jit(solution)/shard_map/cond
  1986.7 69.0 %collective-permute-start.7 = (bf16[512,1024]{1,0:T(8,128)(2,1)}, bf16[512,1024]{1,0:T(8,128)(2,1)S(1)}, u32[]{:S(2)}, u32[]{:S(2)}) collective-permute-start(bf16[512,1024]{1,0:T(8,128)(2,1)} %get-tuple-element.807), channel_id=1, source_target_pairs={{8,0},{16,8},{24,16},{9,1},{17,9},{25,17},{10,2},{18,10},{26,18},{... | collective-permute-start | bytes 3145736 | tf_op jit(solution)/shard_map/ppermute | solution.py:30
  2058.3 40.5 %copy-start.95 = (pred[512,512]{0,1:T(8,128)(4,1)}, pred[512,512]{0,1:T(8,128)(4,1)S(1)}, u32[]{:S(2)}) copy-start(pred[512,512]{0,1:T(8,128)(4,1)S(1)} %fusion.926) | copy-start | bytes 786436 | tf_op jit(solution)/shard_map/cond
  2213.1 63.2 %copy-start.33 = (bf16[512,1024]{1,0:T(8,128)(2,1)}, bf16[512,1024]{1,0:T(8,128)(2,1)S(1)}, u32[]{:S(2)}) copy-start(bf16[512,1024]{1,0:T(8,128)(2,1)S(1)} %get-tuple-element.808) | copy-start | bytes 3145732
  2306.3 17.5 copy-start.34
  (30 other events, 111.7 us)
Sparse Core Ops, SparseCore 0:
  12.6 295.0 all-gather.1
  2276.5 652.2 all-reduce.12
where the time goes:
time: 2950 us; the launch traced here: 2940 us
  waiting for transfers between devices  1650 us (56%)
  other arithmetic  460 us (16%)
  loops' own time  271 us (9%)
  matrix products  248 us (8%)
  local copies, waits for them, and re-layouts  191 us (6%)
  starting transfers between devices  93.3 us (3%)
    ppermute x8, waiting for transfers between devices, passed_along(): lax.ppermute(value, axis, [(source, source + steps) for source in range(i...  753 us
    unnamed x3, waiting for transfers between devices  604 us
    all_gather x1, other arithmetic, per_device(): gathered = lax.all_gather(shard_low, 'dp', axis=1, tiled=True)[0]  358 us
    all_gather x1, waiting for transfers between devices, per_device(): gathered = lax.all_gather(shard_low, 'dp', axis=1, tiled=True)[0]  291 us
    another operation x5, loops' own time, per_device(): lax.switch(branch_index, backward_fns, back_weights, residual, seg_ids, g...  155 us
    another operation x5, loops' own time, per_device(): result = lax.switch(branch_index, forward_fns, gathered, residual, seg_ids)  115 us
    ppermute x8, starting transfers between devices, passed_along(): lax.ppermute(value, axis, [(source, source + steps) for source in range(i...  93.2 us
    slice x24, local copies, waits for them, and re-layouts, unpack(): flat_vec[offset:offset + row_count * col_count]  71.2 us
  transfers between devices with their start and end apart: 10, of which 10 were waited for; matrix products, arithmetic and copies ran while one was open for 1% of the time, Pallas kernels for 0%

commit v1 on v0

--- a/solution.py
+++ b/solution.py
@@ -2,7 +2,10 @@
 
 import jax
 import jax.numpy as jnp
+import numpy as np
 from jax import lax
+from jax.experimental import pallas as pl
+from jax.experimental.pallas import tpu as pltpu
 from jax.sharding import PartitionSpec as P
 
 D = 1024
@@ -433,21 +436,969 @@
     return (produced[None], grads_in[None], shard_total, gain_grads)
 
 
+AXES = ("y", "x", "z", "c")
+GROUP = ("y", "z", "c")
+DEPTH = 4
+WIDE = 1408
+TILE = 128
+STRETCHES = ((0, 172, 176), (688, 258, 264), (1720, 258, 264))
+bf16 = jnp.bfloat16
+f32 = jnp.float32
+
+
+def unit_columns(half):
+    order = []
+    for first, count, padded in STRETCHES:
+        for part in (2 * half, 2 * half + 1):
+            start = first + count * part
+            order += list(range(start, start + count)) + [-1] * (padded - count)
+    return order
+
+
+COLUMNS = np.array(unit_columns(0) + unit_columns(1), np.int32)
+
+
+def route(value, rule):
+    pairs = []
+    for y in range(2):
+        for x in range(2):
+            for z in range(DEPTH):
+                for c in range(2):
+                    target = rule(y, x, z, c)
+                    if target is not None:
+                        ty, tx, tz, tc = target
+                        pairs.append((((2 * y + x) * DEPTH + z) * 2 + c, ((2 * ty + tx) * DEPTH + tz) * 2 + tc))
+    return lax.ppermute(value, AXES, pairs)
+
+
+def swap_x(value):
+    return route(value, lambda y, x, z, c: (y, 1 - x, z, c))
+
+
+def swap_y(value):
+    return route(value, lambda y, x, z, c: (1 - y, x, z, c))
+
+
+def swap_xy(value):
+    return route(value, lambda y, x, z, c: (1 - y, 1 - x, z, c))
+
+
+def swap_c(value):
+    return route(value, lambda y, x, z, c: (y, x, z, 1 - c))
+
+
+def along_z(value, moves):
+    return route(value, lambda y, x, z, c: (y, x, moves[z], c) if z in moves else None)
+
+
+def spot(y, z, c):
+    return (y * DEPTH + z) * 2 + c
+
+
+def by_index(index, choices):
+    result = choices[-1]
+    for i in range(len(choices) - 2, -1, -1):
+        result = jnp.where(index == i, choices[i], result)
+    return result
+
+
+def tied(*values):
+    spec = pl.BlockSpec(memory_space=pl.ANY)
+    return pl.pallas_call(
+        lambda *refs: None,
+        in_specs=[spec] * len(values),
+        out_specs=[spec] * len(values),
+        out_shape=[jax.ShapeDtypeStruct(value.shape, value.dtype) for value in values],
+        input_output_aliases={i: i for i in range(len(values))},
+    )(*values)
+
+
+def lane_mask(width, lanes, index):
+    return (lax.broadcasted_iota(jnp.int32, (1, lanes), 1) // width) == index
+
+
+def dot_nt(a, b):
+    return lax.dot_general(a, b, (((1,), (1,)), ((), ())), preferred_element_type=f32)
+
+
+def dot_tn(a, b):
+    return lax.dot_general(a, b, (((0,), (0,)), ((), ())), preferred_element_type=f32)
+
+
+def pair_mask(row_seg, col_seg, row_start, rows, key_start, keys, window):
+    query_pos = row_start + lax.broadcasted_iota(jnp.int32, (rows, keys), 0)
+    key_pos = key_start + lax.broadcasted_iota(jnp.int32, (rows, keys), 1)
+    allowed = (key_pos <= query_pos) & (
+        col_seg[row_start : row_start + rows, :] == row_seg[:, key_start : key_start + keys]
+    )
+    if window:
+        allowed = allowed & (query_pos - key_pos < window)
+    return allowed
+
+
+def tiles(taylor, row_total):
+    step = 256 if taylor else 128
+    reach = row_total if taylor else 128
+    return [(start, step, max(0, start - reach)) for start in range(0, row_total, step)]
+
+
+def probabilities(taylor, score, allowed):
+    if taylor:
+        poly = jnp.where(allowed, 1.0 + score + 0.5 * score * score, 0.0)
+        inv_total = 1.0 / jnp.sum(poly, axis=-1, keepdims=True)
+        return poly * inv_total, inv_total
+    masked = jnp.where(allowed, score, NEG_LARGE)
+    expo = jnp.where(allowed, jnp.exp(masked - jnp.max(masked, axis=-1, keepdims=True)), 0.0)
+    inv_total = 1.0 / jnp.sum(expo, axis=-1, keepdims=True)
+    return expo * inv_total, inv_total
+
+
+def mix_kernel(taylor, row_seg_ref, col_seg_ref, q_ref, k_ref, v_ref, out_ref):
+    row_seg, col_seg = row_seg_ref[...], col_seg_ref[...]
+    row_total = q_ref.shape[0]
+    for start, rows, first in tiles(taylor, row_total):
+        keys = start + rows - first
+        allowed = pair_mask(row_seg, col_seg, start, rows, first, keys, 0 if taylor else WINDOW)
+        for pair in range(v_ref.shape[1] // 128):
+            lanes = slice(128 * pair, 128 * pair + 128)
+            narrow = slice(0, 128) if taylor else lanes
+            outs = []
+            for j in range(2):
+                qk_mask = lane_mask(16, 128, 2 * pair + j) if taylor else lane_mask(64, 128, j)
+                q = jnp.where(qk_mask, q_ref[start : start + rows, narrow], 0).astype(bf16)
+                score = dot_nt(q, k_ref[first : first + keys, narrow]) * (0.25 if taylor else 0.125)
+                probs, _ = probabilities(taylor, score, allowed)
+                outs.append(
+                    jnp.dot(probs.astype(bf16), v_ref[first : first + keys, lanes], preferred_element_type=f32)
+                )
+            out_ref[start : start + rows, lanes] = jnp.where(lane_mask(64, 128, 0), outs[0], outs[1]).astype(bf16)
+
+
+def mix_grad_kernel(
+    taylor, row_seg_ref, col_seg_ref, q_ref, k_ref, v_ref, gm_ref, gq_ref, gk_ref, gv_ref, aq, ak, av
+):
+    row_seg, col_seg = row_seg_ref[...], col_seg_ref[...]
+    row_total = q_ref.shape[0]
+    scale = 0.25 if taylor else 0.125
+    aq[...] = jnp.zeros_like(aq)
+    ak[...] = jnp.zeros_like(ak)
+    av[...] = jnp.zeros_like(av)
+    for start, rows, first in tiles(taylor, row_total):
+        stop = start + rows
+        keys = stop - first
+        allowed = pair_mask(row_seg, col_seg, start, rows, first, keys, 0 if taylor else WINDOW)
+        for pair in range(v_ref.shape[1] // 128):
+            lanes = slice(128 * pair, 128 * pair + 128)
+            narrow = slice(0, 128) if taylor else lanes
+            for j in range(2):
+                qk_mask = lane_mask(16, 128, 2 * pair + j) if taylor else lane_mask(64, 128, j)
+                q = jnp.where(qk_mask, q_ref[start:stop, narrow], 0).astype(bf16)
+                k = jnp.where(qk_mask, k_ref[first:stop, narrow], 0).astype(bf16)
+                gm = jnp.where(lane_mask(64, 128, j), gm_ref[start:stop, lanes], 0).astype(bf16)
+                score = dot_nt(q, k) * scale
+                probs, inv_total = probabilities(taylor, score, allowed)
+                grad_probs = dot_nt(gm, v_ref[first:stop, lanes])
+                centred = grad_probs - jnp.sum(grad_probs * probs, axis=-1, keepdims=True)
+                if taylor:
+                    grad_score = jnp.where(allowed, centred * (1.0 + score) * inv_total, 0.0)
+                else:
+                    grad_score = probs * centred
+                grad_score = grad_score.astype(bf16)
+                aq[start:stop, narrow] += jnp.dot(grad_score, k, preferred_element_type=f32) * scale
+                ak[first:stop, narrow] += dot_tn(grad_score, q) * scale
+                av[first:stop, lanes] += dot_tn(probs.astype(bf16), gm)
+    gq_ref[...] = aq[...].astype(bf16)
+    gk_ref[...] = ak[...].astype(bf16)
+    gv_ref[...] = av[...].astype(bf16)
+
+
+def mix(taylor, seg_ids, q, k, v):
+    return pl.pallas_call(
+        partial(mix_kernel, taylor),
+        in_specs=[pl.BlockSpec(memory_space=pltpu.VMEM)] * 5,
+        out_shape=jax.ShapeDtypeStruct(v.shape, bf16),
+        compiler_params=pltpu.CompilerParams(vmem_limit_bytes=32 * 2**20),
+        cost_estimate=pl.CostEstimate(flops=2**30, bytes_accessed=2**21, transcendentals=0),
+    )(seg_ids[None, :], seg_ids[:, None], q, k, v)
+
+
+def mix_grad(taylor, seg_ids, q, k, v, gm):
+    return pl.pallas_call(
+        partial(mix_grad_kernel, taylor),
+        in_specs=[pl.BlockSpec(memory_space=pltpu.VMEM)] * 6,
+        out_shape=[jax.ShapeDtypeStruct(a.shape, bf16) for a in (q, k, v)],
+        scratch_shapes=[pltpu.VMEM(a.shape, f32) for a in (q, k, v)],
+        compiler_params=pltpu.CompilerParams(vmem_limit_bytes=32 * 2**20),
+        cost_estimate=pl.CostEstimate(flops=3 * 2**30, bytes_accessed=2**22, transcendentals=0),
+    )(seg_ids[None, :], seg_ids[:, None], q, k, v, gm)
+
+
+SHARD = 8257
+LINED = 8256
+LEFT = 192
+UNIT = 1024
+ROWS = 2176
+GAIN = 16
+PAIR = 43
+
+
+def pieces(position, count, table):
+    found = []
+    for place in range(count):
+        number = int(table[position + place])
+        if number < 0:
+            continue
+        if found and found[-1][1] == place and found[-1][2] + place - found[-1][0] == number:
+            found[-1][1] = place + 1
+        else:
+            found.append([place, place + 1, number])
+    return found
+
+
+def shifted(load, position, last):
+    row, shift = position // TILE, position % TILE
+    near = load(min(max(row, 0), last))
+    if shift == 0:
+        return near
+    far = load(min(max(row + 1, 0), last))
+    lane = lax.broadcasted_iota(jnp.int32, near.shape, 1)
+    return pltpu.roll(jnp.where(lane >= shift, near, far), TILE - shift, 1)
+
+
+def between_lanes(shape, low, high):
+    lane = lax.broadcasted_iota(jnp.int32, shape, 1)
+    return (lane >= low) & (lane < high)
+
+
+def masked_rows(value, rows):
+    row = lax.broadcasted_iota(jnp.int32, value.shape, 0)
+    return jnp.where(row < rows, value, 0.0)
+
+
+def unit_stretches(owner_y, d, half):
+    if owner_y == 1:
+        if d == 3:
+            return [(512 * half, 0, 1), (512 * half, 4, 1)]
+        return [(0, 4 * half, 1), (512, 4 * half, 1)]
+    if d == 0:
+        return [(0, half, 2), (512, 4 * half, 1)]
+    if d == 1:
+        return [(0, 4 * half, 1), None]
+    return [(0, 0, 1), (0, 4, 1)] if half else [None, None]
+
+
+UNIT_CASES = [
+    (1, 0, lambda y, d: (y == 1) & (d < 3)),
+    (1, 3, lambda y, d: (y == 1) & (d == 3)),
+    (0, 0, lambda y, d: (y == 0) & (d == 0)),
+    (0, 1, lambda y, d: (y == 0) & (d == 1)),
+    (0, 2, lambda y, d: (y == 0) & (d == 2)),
+]
+
+
+def source_kernel(info_ref, flat_ref, left_ref, right_ref, out_ref, moved_ref, buf, column, sem):
+    copy = pltpu.make_async_copy(flat_ref.reshape(SHARD, TILE), buf.at[pl.ds(LEFT, SHARD)], sem)
+    copy.start()
+    buf[:LEFT, :] = left_ref[...]
+    copy.wait()
+    buf[LEFT + SHARD : LEFT + SHARD + 8, :] = right_ref[...]
+    start, x, y, d = info_ref[0], info_ref[1], info_ref[2], info_ref[3]
+    gain = buf[LEFT : LEFT + GAIN, :].astype(bf16)
+
+    for owner_y, unit_d, chosen in UNIT_CASES:
+
+        @pl.when((x == 0) & chosen(y, d))
+        def _(owner_y=owner_y, unit_d=unit_d):
+            for half in range(2):
+                for k in range(4):
+                    part, deep = k % 2, k // 2
+                    place, base = half * 2 + (part ^ owner_y), deep * (UNIT + GAIN)
+                    for side, stretch in enumerate(unit_stretches(owner_y, unit_d, half)):
+                        if stretch is not None:
+                            row, strip, step = stretch
+                            value = buf[pl.ds(start + 8 * row + strip + step * k, 512, stride=8), :]
+                            out_ref[place, base + 512 * side : base + 512 * side + 512, :] = value.astype(bf16)
+                    out_ref[place, base + UNIT : base + UNIT + GAIN, :] = gain
+            if (owner_y, unit_d) == (0, 1):
+                for k in range(4):
+                    for side in range(2):
+                        value = buf[pl.ds(start + 8 * 512 + 4 * side + k, 512, stride=8), :]
+                        row = (k // 2) * (UNIT + GAIN) + 512 * side
+                        moved_ref[k % 2, row : row + 512, :] = value.astype(bf16)
+
+    @pl.when((x == 1) & (d <= 5))
+    def _():
+        for half in range(2):
+            for j in range(WIDE // TILE):
+                for parity in range(2):
+                    load = lambda row: buf[pl.ds(start + row, 192, stride=PAIR), :]
+                    value = jnp.zeros((192, TILE), f32)
+                    for low, high, number in pieces(WIDE * half + TILE * j, TILE, COLUMNS):
+                        got = shifted(load, parity * FF + number - low, PAIR)
+                        value = jnp.where(between_lanes(value.shape, low, high), got, value)
+                    column[pl.ds(parity, 192, stride=2), :] = value
+                whole = column[...].astype(bf16)
+
+                @pl.when(d <= 4)
+                def _():
+                    for r in range(3):
+                        t = 11 * r + j
+                        part, place = (0, t) if t < 17 else (1, t - 17)
+                        out_ref[(1 - half) * 2 + (y ^ part), TILE * place : TILE * place + TILE, :] = whole[
+                            TILE * r : TILE * r + TILE
+                        ]
+
+                @pl.when(d == 5)
+                def _():
+                    part, place = (0, j) if j < 6 else (1, j - 6)
+                    out_ref[(1 - half) * 2 + (y ^ part), TILE * place : TILE * place + TILE, :] = whole[:TILE]
+
+    @pl.when(x == 1)
+    def _():
+        for half in range(2):
+            for part in range(2):
+                q, place = 2 * half + part, (1 - half) * 2 + (y ^ part)
+                out_ref[place, ROWS : ROWS + GAIN, :] = gain
+
+                @pl.when(d == 5)
+                def _():
+                    for j in range(8):
+                        value = buf[pl.ds(start + 8 * (344 + 172 * q) + j, 176, stride=8), :]
+                        first = (6, 5)[part] * TILE + 176 * j
+                        out_ref[place, first : first + 176, :] = masked_rows(value, 172).astype(bf16)
+
+                @pl.when(d > 5)
+                def _():
+                    for j in range(8):
+                        value = buf[pl.ds(start + 8 * 258 * q + j, 272, stride=8), :]
+                        out_ref[place, 272 * j : 272 * j + 272, :] = masked_rows(value, 258).astype(bf16)
+
+
+def line_kernel(info_ref, *refs):
+    block_refs, moved_refs, out_ref, halves = refs[:4], refs[4:6], refs[8], refs[9]
+    x, y, d = info_ref[0], info_ref[1], info_ref[2]
+
+    @pl.when(x == 0)
+    def _():
+        out_ref[...] = jnp.zeros_like(out_ref)
+
+    for owner_y, unit_d, chosen in UNIT_CASES:
+
+        @pl.when((x == 0) & chosen(y, d))
+        def _(owner_y=owner_y, unit_d=unit_d):
+            for half in range(2):
+                for k in range(4):
+                    part, deep = k % 2, k // 2
+                    ref, base = block_refs[half * 2 + (part ^ owner_y)], UNIT * deep
+                    for side, stretch in enumerate(unit_stretches(owner_y, unit_d, half)):
+                        if stretch is not None:
+                            row, strip, step = stretch
+                            value = ref[base + 512 * side : base + 512 * side + 512, :].astype(f32)
+                            out_ref[pl.ds(8 * row + strip + step * k, 512, stride=8), :] = value
+            if (owner_y, unit_d) == (0, 1):
+                for k in range(4):
+                    for side in range(2):
+                        row = UNIT * (k // 2) + 512 * side
+                        value = moved_refs[k % 2][row : row + 512, :].astype(f32)
+                        out_ref[pl.ds(8 * 512 + 4 * side + k, 512, stride=8), :] = value
+
+    inverse = np.full((2 * FF,), -1, np.int64)
+    for place, number in enumerate(COLUMNS):
+        if number >= 0:
+            inverse[number] = place
+            inverse[FF + number] = 2 * WIDE + place
+
+    for own_y in range(2):
+
+        @pl.when((x == 1) & (d <= 5) & (y == own_y))
+        def _(own_y=own_y):
+            for half in range(2):
+                ref = [block_refs[(1 - half) * 2 + (part ^ own_y)] for part in range(2)]
+
+                @pl.when(d <= 4)
+                def _():
+                    for t in range(33):
+                        part, place = (0, t) if t < 17 else (1, t - 17)
+                        r, j = t // 11, t % 11
+                        halves[11 * half + j, TILE * r : TILE * r + TILE, :] = ref[part][
+                            TILE * place : TILE * place + TILE, :
+                        ].astype(f32)
+
+                @pl.when(d == 5)
+                def _():
+                    for j in range(11):
+                        part, place = (0, j) if j < 6 else (1, j - 6)
+                        halves[11 * half + j, :TILE, :] = ref[part][
+                            TILE * place : TILE * place + TILE, :
+                        ].astype(f32)
+
+    @pl.when((x == 1) & (d <= 5))
+    def _():
+        for b in range(PAIR):
+            value = jnp.zeros((192, TILE), f32)
+            for low, high, number in pieces(TILE * b, TILE, inverse):
+                parity, rest = number // (2 * WIDE), number % (2 * WIDE)
+                half, local = rest // WIDE, rest % WIDE
+                load = lambda j: halves[11 * half + j, pl.ds(parity, 192, stride=2), :]
+                got = shifted(load, local - low, WIDE // TILE - 1)
+                value = jnp.where(between_lanes(value.shape, low, high), got, value)
+            out_ref[pl.ds(b, 192, stride=PAIR), :] = value
+
+    for own_y in range(2):
+
+        @pl.when((x == 1) & (d >= 5) & (y == own_y))
+        def _(own_y=own_y):
+            for q in range(4):
+                half, part = q // 2, q % 2
+                ref = block_refs[(1 - half) * 2 + (part ^ own_y)]
+
+                @pl.when(d == 5)
+                def _():
+                    for j in range(8):
+                        first = (6, 5)[part] * TILE + 176 * j
+                        value = ref[first : first + 176, :].astype(f32)
+                        out_ref[pl.ds(8 * (344 + 172 * q) + j, 176, stride=8), :] = value
+
+                @pl.when(d > 5)
+                def _():
+                    for j in range(8):
+                        value = ref[272 * j : 272 * j + 272, :].astype(f32)
+                        out_ref[pl.ds(8 * 258 * q + j, 264, stride=8), :] = value[:264]
+
+
+def flat_kernel(start_ref, lined_ref, left_ref, right_ref, out_ref, buf, staged, sem):
+    buf[:8, :] = left_ref[...]
+    buf[8 : 8 + LINED, :] = lined_ref[:LINED, :]
+    buf[8 + LINED :, :] = jnp.zeros((buf.shape[0] - 8 - LINED, 128), f32)
+
+    @pl.when(start_ref[1] == 0)
+    def _():
+        buf[8 + 8192 : 8 + 8192 + 256, :] = right_ref[...]
+
+    staged[...] = buf[pl.ds(start_ref[0], SHARD), :]
+    copy = pltpu.make_async_copy(staged, out_ref.reshape(SHARD, 128), sem)
+    copy.start()
+    copy.wait()
+
+
+def padded(m, rows):
+    return jnp.pad(m, ((0, rows - m.shape[0]), (0, 0)))
+
+
+def dp_right(value):
+    return lax.ppermute(value, AXES, [(8 * s + i, 8 * s + i + 1) for s in range(4) for i in range(7)])
+
+
+def dp_left(value):
+    return lax.ppermute(value, AXES, [(8 * s + i + 1, 8 * s + i) for s in range(4) for i in range(7)])
+
+
+def source_blocks(flat_params, y, x, z, c, d):
+    tail = flat_params[:, -LEFT * 128 :].reshape(LEFT, 128)
+    head = flat_params[:, :1024].reshape(8, 128)
+    left, right = dp_right(tail), dp_left(head)
+    start = jnp.maximum(200 - jnp.where(x == 0, 65 * d, d), 0)
+    blocks, moved = pl.pallas_call(
+        source_kernel,
+        in_specs=[
+            pl.BlockSpec(memory_space=pltpu.SMEM),
+            pl.BlockSpec(memory_space=pl.ANY),
+            pl.BlockSpec(memory_space=pltpu.VMEM),
+            pl.BlockSpec(memory_space=pltpu.VMEM),
+        ],
+        out_shape=[
+            jax.ShapeDtypeStruct((4, ROWS + GAIN, TILE), bf16),
+            jax.ShapeDtypeStruct((2, ROWS + GAIN, TILE), bf16),
+        ],
+        scratch_shapes=[pltpu.VMEM((8576, TILE), f32), pltpu.VMEM((384, TILE), f32), pltpu.SemaphoreType.DMA],
+        compiler_params=pltpu.CompilerParams(vmem_limit_bytes=40 * 2**20),
+    )(jnp.stack([start, x, y, d]), flat_params, left, right)
+    moved = route(moved, lambda yy, xx, zz, cc: (0, 0, 1, 0) if (yy, xx, zz, cc) == (0, 0, 0, 1) else None)
+    from_x, from_xy = swap_x(blocks[2]), swap_xy(blocks[3])
+    swapped = (y == 0) & (x == 0) & (d == 2)
+    own, flipped = jnp.where(swapped, moved[0], blocks[0]), jnp.where(swapped, moved[1], blocks[1])
+    from_y = swap_y(flipped)
+    own_units, own_rows = jnp.where(x == 0, own, from_x), jnp.where(x == 0, from_x, own)
+    other_units, other_rows = jnp.where(x == 0, from_y, from_xy), jnp.where(x == 0, from_xy, from_y)
+    size = UNIT + GAIN
+
+    pick = lambda owner, own, other: jnp.where(y == owner, own, other)
+    units = [pick(owner, own_units, other_units) for owner in (0, 1)]
+    ahead = along_z(jnp.stack([unit[size : 2 * size] for unit in units]), {0: 2, 1: 3})
+    units = [jnp.where(z < 2, unit[:size], later) for unit, later in zip(units, ahead)]
+    rows = [pick(owner, own_rows, other_rows) for owner in (0, 1)]
+    return jnp.concatenate([units[0], rows[0], units[1]], axis=0), rows[1]
+
+
+def fetch(places, gathered_refs, blocks, sems):
+    copies, done = [], 0
+    for i, ((first, rows), ref) in enumerate(zip(places, gathered_refs)):
+        for p in range(16):
+            target = blocks.at[p, pl.ds(done, rows)]
+            copies.append(pltpu.make_async_copy(ref.at[p, pl.ds(first, rows)], target, sems.at[16 * i + p]))
+        done += rows
+    for copy in copies:
+        copy.start()
+    return copies
+
+
+def unit_weights_kernel(section, places, gathered_ref, _, *refs):
+    *out_refs, gain_ref, blocks, wide, sems = refs
+    for copy in fetch(places, [gathered_ref], blocks, sems):
+        copy.wait()
+    owner = section // 2
+    gain_ref[...] = blocks[spot(owner, 0, 0), UNIT : UNIT + GAIN, :]
+    q_ref, k_ref, v_ref, o_ref = out_refs
+    for k in range(4):
+        block = lambda d, low, high: blocks[spot(k % 2, d // 2 + 2 * (k // 2), d % 2), low:high, :]
+        lanes = slice(128 * k, 128 * k + 128)
+        far = slice(512 + 128 * k, 512 + 128 * k + 128)
+        if section:
+            q_ref[:, lanes] = block(0, 0, 1024)
+            k_ref[:, lanes] = block(1, 0, 1024)
+            v_ref[:, lanes] = block(2, 0, 1024)
+            o_ref[:, lanes] = block(3, 0, 512)
+            o_ref[:, far] = block(3, 512, 1024)
+        else:
+            wide[0, pl.ds(k, 256, stride=4), :] = block(0, 0, 256).astype(f32)
+            wide[1, pl.ds(k, 256, stride=4), :] = block(0, 256, 512).astype(f32)
+            v_ref[:512, lanes] = block(0, 512, 1024)
+            v_ref[512:, lanes] = block(1, 0, 512)
+            o_ref[:, lanes] = block(2, 0, 512)
+            o_ref[:, far] = block(2, 512, 1024)
+    if section == 0:
+        q_ref[...] = wide[0].astype(bf16)
+        k_ref[...] = wide[1].astype(bf16)
+
+
+def unit_weights(section, earlier, places, *gathered):
+    narrow = (D, 512 if section else 128)
+    shapes = [narrow, narrow, (D, 512), (512, D), (GAIN, TILE)]
+    *weights, gain = pl.pallas_call(
+        partial(unit_weights_kernel, section, places),
+        in_specs=[pl.BlockSpec(memory_space=pltpu.HBM), pl.BlockSpec(memory_space=pl.ANY)],
+        out_shape=[jax.ShapeDtypeStruct(shape, bf16) for shape in shapes],
+        scratch_shapes=[
+            pltpu.VMEM((16, UNIT + GAIN, TILE), bf16),
+            pltpu.VMEM((2, 1024, TILE), f32),
+            pltpu.SemaphoreType.DMA((16,)),
+        ],
+        compiler_params=pltpu.CompilerParams(vmem_limit_bytes=40 * 2**20),
+    )(*gathered, earlier)
+    return gain[:8].reshape(1, D).astype(f32), tuple(weights)
+
+
+def row_places():
+    places = []
+    for d in range(6):
+        for part, count, skipped in ((0, 17 if d < 5 else 6, 0), (1, 16 if d < 5 else 5, 17 if d < 5 else 6)):
+            places.append((spot(part, d // 2, d % 2), 33 * d + skipped, count))
+    return places
+
+
+def strip_places():
+    places = [(spot(part, 2, 1), (6, 5)[part] * TILE, 176, 176 * part, 176) for part in (0, 1)]
+    for i in range(4):
+        places.append((spot(i % 2, 3, i // 2), 0, 272, 352 + 264 * i, 264))
+    return places
+
+
+def row_weights_kernel(section, places, *refs):
+    gathered_refs = refs[: len(places)]
+    gate_ref, up_ref, down_ref, gain_ref, blocks, wide, sems = refs[len(places) + 1 :]
+    for copy in fetch(places, gathered_refs, blocks, sems):
+        copy.wait()
+    gain_ref[...] = blocks[spot(section // 2, 0, 0), ROWS : ROWS + GAIN, :]
+    for p, start, count in row_places():
+        for i in range(count):
+            r, j = (start + i) // 11, (start + i) % 11
+            ref = gate_ref if r < 8 else up_ref
+            ref[TILE * (r % 8) : TILE * (r % 8) + TILE, TILE * j : TILE * j + TILE] = blocks[
+                p, TILE * i : TILE * i + TILE, :
+            ]
+    for p, start, step, unit, count in strip_places():
+        for j in range(8):
+            value = blocks[p, start + step * j : start + step * j + step, :].astype(f32)
+            wide[unit : unit + count, TILE * j : TILE * j + TILE] = value[:count]
+    down_ref[...] = wide[...].astype(bf16)
+
+
+def row_weights(section, earlier, places, *gathered):
+    shapes = [(D, WIDE), (D, WIDE), (WIDE, D), (GAIN, TILE)]
+    *weights, gain = pl.pallas_call(
+        partial(row_weights_kernel, section, places),
+        in_specs=[pl.BlockSpec(memory_space=pltpu.HBM)] * len(places) + [pl.BlockSpec(memory_space=pl.ANY)],
+        out_shape=[jax.ShapeDtypeStruct(shape, bf16) for shape in shapes],
+        scratch_shapes=[
+            pltpu.VMEM((16, ROWS + GAIN, TILE), bf16),
+            pltpu.VMEM((WIDE, D), f32),
+            pltpu.SemaphoreType.DMA((16 * len(places),)),
+        ],
+        compiler_params=pltpu.CompilerParams(vmem_limit_bytes=48 * 2**20),
+    )(*gathered, earlier)
+    return gain[:8].reshape(1, D).astype(f32), tuple(weights)
+
+
+def halves_of(refs):
+    if len(refs) == 2:
+        return refs
+    rows = refs[0].shape[0] // 2
+    return refs[0].at[:rows], refs[0].at[rows:]
+
+
+def dot_rows(first, lanes, second):
+    return sum(dot_tn(a[:, lanes], b[...]) for a, b in zip(first, second))
+
+
+def grouped(counts, refs):
+    groups, at = [], 0
+    for count in counts:
+        group = refs[at : at + count]
+        groups.append(group if len(set(counts)) == 1 else halves_of(group))
+        at += count
+    return groups, refs[at:]
+
+
+def pack_rows_kernel(counts, *refs):
+    (hidden, gate, up, activ, grad), refs = grouped(counts, refs)
+    _, out_ref, done_ref, wide = refs
+    done_ref[...] = jnp.zeros_like(done_ref)
+    place_of = {}
+    for p, start, count in row_places():
+        for i in range(count):
+            place_of[start + i] = (p, i)
+    for side, local in enumerate((gate, up)):
+        for first in (0, 512):
+            value = dot_rows(hidden, slice(first, first + 512), local).astype(bf16)
+            for r in range(4):
+                for j in range(11):
+                    p, i = place_of[11 * (8 * side + first // TILE + r) + j]
+                    out_ref[p, TILE * i : TILE * i + TILE, :] = value[
+                        TILE * r : TILE * r + TILE, TILE * j : TILE * j + TILE
+                    ]
+    for first, count in ((0, 512), (512, 512), (1024, 384)):
+        wide[first : first + count, :] = dot_rows(activ, slice(first, first + count), grad)
+    wide[WIDE:, :] = jnp.zeros((8, D), f32)
+    for p, start, step, unit, _ in strip_places():
+        for j in range(8):
+            value = wide[unit : unit + step, TILE * j : TILE * j + TILE].astype(bf16)
+            out_ref[p, start + step * j : start + step * j + step, :] = value
+
+
+def pack_rows(hidden, grad_gate, grad_up, activ, grad, earlier):
+    operands = (hidden, grad_gate, grad_up, activ, grad)
+    counts = [len(operand) for operand in operands]
+    return pl.pallas_call(
+        partial(pack_rows_kernel, counts),
+        in_specs=[pl.BlockSpec(memory_space=pltpu.VMEM)] * sum(counts) + [pl.BlockSpec(memory_space=pl.ANY)],
+        out_shape=[jax.ShapeDtypeStruct((16, ROWS, TILE), bf16), jax.ShapeDtypeStruct((8, TILE), f32)],
+        scratch_shapes=[pltpu.VMEM((WIDE + 8, D), f32)],
+        compiler_params=pltpu.CompilerParams(vmem_limit_bytes=48 * 2**20),
+        cost_estimate=pl.CostEstimate(flops=2 * 512 * 3 * D * WIDE, bytes_accessed=2**24, transcendentals=0),
+    )(*sum(map(list, operands), []), earlier)
+
+
+def pack_units_kernel(section, counts, info_ref, *refs):
+    y, z, c = info_ref[0], info_ref[1], info_ref[2]
+    (hidden, grad, gq, gk, gv, mixed), refs = grouped(counts, refs)
+    _, out_ref, done_ref, *scratch = refs
+    done_ref[...] = jnp.zeros_like(done_ref)
+
+    def store(d, k, low, high, value):
+        base = UNIT * (k // 2)
+        out_ref[c ^ (d % 2), y ^ (k % 2), (d // 2) ^ (z & 1), base + low : base + high, :] = value
+
+    if section:
+        for d, local in enumerate((gq, gk, gv)):
+            for r in range(4):
+                value = dot_rows(hidden, slice(256 * r, 256 * r + 256), local).astype(bf16)
+                for k in range(4):
+                    store(d, k, 256 * r, 256 * r + 256, value[:, 128 * k : 128 * k + 128])
+        out_d = 3
+    else:
+        (wide,) = scratch
+        for d, local in enumerate((gq, gk)):
+            for r in range(4):
+                wide[d, 256 * r : 256 * r + 256, :] = dot_rows(hidden, slice(256 * r, 256 * r + 256), local)
+            for k in range(4):
+                store(0, k, 256 * d, 256 * d + 256, wide[d, pl.ds(k, 256, stride=4), :].astype(bf16))
+        for r in range(4):
+            value = dot_rows(hidden, slice(256 * r, 256 * r + 256), gv).astype(bf16)
+            for k in range(4):
+                low = (512, 768, 0, 256)[r]
+                store(0 if r < 2 else 1, k, low, low + 256, value[:, 128 * k : 128 * k + 128])
+        for k in range(4):
+            store(1, k, 512, 1024, jnp.zeros((512, TILE), bf16))
+            store(3, k, 0, 1024, jnp.zeros((1024, TILE), bf16))
+        out_d = 2
+    for r in range(2):
+        value = dot_rows(mixed, slice(256 * r, 256 * r + 256), grad).astype(bf16)
+        for k in range(8):
+            low = 512 * (k // 4) + 256 * r
+            store(out_d, k % 4, low, low + 256, value[:, 128 * k : 128 * k + 128])
+
+
+def pack_units(section, place, hidden, gq, gk, gv, mixed, grad, earlier):
+    operands = (hidden, grad, [gq], [gk], [gv], [mixed])
+    counts = [len(operand) for operand in operands]
+    return pl.pallas_call(
+        partial(pack_units_kernel, section, counts),
+        in_specs=[pl.BlockSpec(memory_space=pltpu.SMEM)]
+        + [pl.BlockSpec(memory_space=pltpu.VMEM)] * sum(counts)
+        + [pl.BlockSpec(memory_space=pl.ANY)],
+        out_shape=[jax.ShapeDtypeStruct((2, 2, 2, 2 * UNIT, TILE), bf16), jax.ShapeDtypeStruct((8, TILE), f32)],
+        scratch_shapes=[] if section else [pltpu.VMEM((2, UNIT, TILE), f32)],
+        compiler_params=pltpu.CompilerParams(vmem_limit_bytes=40 * 2**20),
+        cost_estimate=pl.CostEstimate(flops=2 * 512 * 4 * D * 512, bytes_accessed=2**23, transcendentals=0),
+    )(place, *sum(map(list, operands), []), earlier)
+
+
+def add(first, second):
+    return (first.astype(f32) + second.astype(f32)).astype(bf16)
+
+
+def scattered(blocks):
+    return lax.psum_scatter(blocks, GROUP, scatter_dimension=0, tiled=False)
+
+
+def param_shard(units, rows, gain, place_rows, received, y, x, z, c, d):
+    pick = lambda owner, pair: jnp.where(y == owner, pair[0], pair[1])
+    units = [padded(unit, ROWS) for unit in units]
+    own_units, other_units = pick(0, units), pick(1, units)
+    own_rows, other_rows = pick(0, rows), pick(1, rows)
+    from_x = swap_x(jnp.where(x == 0, own_rows, own_units))
+    from_xy = swap_xy(jnp.where(x == 0, other_rows, other_units))
+    from_y = swap_y(jnp.where(x == 0, other_units, other_rows))
+    from_x, gain, *sent, got_out, got_grad = tied(from_x, gain, own_units, other_units, *received)
+    results = place_rows((got_out, got_grad))
+    gain = gain + along_z(gain, {0: 2, 2: 0, 1: 3, 3: 1})
+    gain_own = lax.dynamic_index_in_dim(gain, 2 * y + x, 0, keepdims=True)
+    own = jnp.where(x == 0, own_units, own_rows)
+    moved = [
+        route(block, lambda yy, xx, zz, cc: (0, 0, 0, 1) if (yy, xx, zz, cc) == (source, 0, 1, 0) else None)
+        for source, block in enumerate(sent)
+    ]
+    lined = pl.pallas_call(
+        line_kernel,
+        in_specs=[pl.BlockSpec(memory_space=pltpu.SMEM)]
+        + [pl.BlockSpec(memory_space=pltpu.VMEM)] * 6
+        + [pl.BlockSpec(memory_space=pl.ANY)] * 2,
+        out_shape=jax.ShapeDtypeStruct((LINED + 64, TILE), f32),
+        scratch_shapes=[pltpu.VMEM((22, 384, TILE), f32)],
+        compiler_params=pltpu.CompilerParams(vmem_limit_bytes=40 * 2**20),
+    )(jnp.stack([x, y, d]), own, from_y, from_x, from_xy, *moved, *results)
+    left = dp_right(jnp.where(x == 0, lined[8184:8192], lined[LINED - 8 : LINED]))
+    right = dp_left(lined[:256])
+    left = jnp.where(d == 0, gain_own.reshape(8, 128), left)
+    start = jnp.where(x == 0, jnp.minimum(65 * d, 263), d)
+    shard = pl.pallas_call(
+        flat_kernel,
+        in_specs=[pl.BlockSpec(memory_space=pltpu.SMEM)] + [pl.BlockSpec(memory_space=pltpu.VMEM)] * 3,
+        out_specs=pl.BlockSpec(memory_space=pl.ANY),
+        out_shape=jax.ShapeDtypeStruct((1, SHARD * 128), f32),
+        scratch_shapes=[pltpu.VMEM((8528, 128), f32), pltpu.VMEM((SHARD, 128), f32), pltpu.SemaphoreType.DMA],
+        compiler_params=pltpu.CompilerParams(vmem_limit_bytes=40 * 2**20),
+    )(jnp.stack([start, x]), lined, left, right)
+    return results, shard, gain_own
+
+
+def mlp_grad(weights, kept, grad):
+    w_gate, w_up, w_down = weights
+    gate, up = kept[3:5]
+    grad_activ = dot_right(grad, w_down)
+    sig = jax.nn.sigmoid(gate)
+    grad_gate = (grad_activ * up * sig * (1.0 + gate * (1.0 - sig))).astype(bf16)
+    grad_up = (grad_activ * gate * sig).astype(bf16)
+    partial_hidden = dot_right(grad_gate, w_gate) + dot_right(grad_up, w_up)
+    return partial_hidden.astype(bf16), (grad_gate, grad_up)
+
+
+def added(entry, *parts):
+    return (entry.astype(f32) + sum(part.astype(f32) for part in parts)).astype(bf16)
+
+
+def per_row(inputs, cotangent, seq_lengths, flat_params):
+    y, x, z, c = (lax.axis_index(axis) for axis in AXES)
+    d = 2 * z + c
+    seg_ids = segment_ids(lax.dynamic_index_in_dim(seq_lengths, y, 0, keepdims=False)[0], inputs.shape[1])
+    block0, block1 = source_blocks(flat_params, y, x, z, c, d)
+    first = lax.all_gather(block0, GROUP)
+    first, block1 = tied(first, block1)
+    second = lax.all_gather(block1, GROUP)
+    unit, rows = UNIT + GAIN, ROWS + GAIN
+    gathered = [([(0, unit)], first), ([(unit, rows)], first), ([(unit + rows, unit)], first), ([(0, rows)], second)]
+    gains, weights, kept, outputs = [None] * 4, [None] * 4, [None] * 4, [None] * 4
+    row_half = inputs.shape[1] // 2
+
+    def cut(rows):
+        return [rows[:row_half], rows[row_half:]]
+
+    def join(halves):
+        return jnp.concatenate(halves, axis=0)
+
+    def open_section(s, earlier):
+        gains[s], weights[s] = (unit_weights if s % 2 == 0 else row_weights)(s, earlier, *gathered[s])
+        kept[s] = []
+        return gains[s]
+
+    def normed_rows(s, entry):
+        hidden, normed, inv_root = norm_forward(entry.astype(f32), gains[s])
+        kept[s].append((hidden.astype(bf16), normed, inv_root))
+        return kept[s][-1][0]
+
+    def heads(s, entry):
+        hidden = normed_rows(s, entry)
+        return [dot_plain(hidden, w).astype(bf16) for w in weights[s][:3]]
+
+    def attention(s, parts):
+        q, k, v = (join(halves) for halves in zip(*parts))
+        mixed = mix(s == 0, seg_ids, q, k, v)
+        kept[s].append((q, k, v, mixed))
+        return [dot_plain(half, weights[s][3]).astype(bf16) for half in cut(mixed)]
+
+    def mlp(s, entry):
+        hidden = normed_rows(s, entry)
+        w_gate, w_up, _ = weights[s]
+        gate = dot_plain(hidden, w_gate)
+        up = dot_plain(hidden, w_up)
+        activ = (jax.nn.silu(gate) * up).astype(bf16)
+        kept[s][-1] += (gate, up, activ)
+        return activ
+
+    entry = cut(lax.dynamic_index_in_dim(inputs, y, 0, keepdims=False))
+    open_section(0, entry[0])
+    branch = attention(0, [heads(0, half) for half in entry])
+    got = [swap_x(half) for half in branch]
+    open_section(1, branch[0])
+    entry[0] = added(entry[0], branch[0], got[0])
+    next_branch = [dot_plain(mlp(1, entry[0]), weights[1][2]).astype(bf16)]
+    got[1], next_branch[0] = tied(got[1], next_branch[0])
+    entry[1] = added(entry[1], branch[1], got[1])
+    outputs[0] = list(entry)
+    next_branch.append(dot_plain(mlp(1, entry[1]), weights[1][2]).astype(bf16))
+    branch = next_branch
+    got = [swap_x(half) for half in branch]
+    open_section(2, branch[1])
+    entry[0] = added(entry[0], branch[0], got[0])
+    first_heads = heads(2, entry[0])
+    got[1], first_heads[0] = tied(got[1], first_heads[0])
+    entry[1] = added(entry[1], branch[1], got[1])
+    outputs[1] = list(entry)
+    branch = join(attention(2, [first_heads, heads(2, entry[1])]))
+    got = swap_x(branch)
+    done = open_section(3, branch)
+    got, _ = tied(got, done)
+
+    grads, gain_sums, sums = [None] * 4, [0.0] * 4, [None] * 4
+    place = jnp.stack([y, z, c])
+
+    def finish(s, half, grad, part, got):
+        grad_hidden = part.astype(f32) + got.astype(f32)
+        _, normed, inv_root = kept[s][half][:3]
+        grad_entry, grad_gain = norm_backward(grad_hidden, gains[s], normed, inv_root)
+        gain_sums[s] += grad_gain
+        return (grad.astype(f32) + grad_entry).astype(bf16)
+
+    def finish_rows(s, grad, parts, got):
+        return [finish(s, half, *rows) for half, rows in enumerate(zip(grad, parts, cut(got)))]
+
+    def pack_mlp(s, local, grad, earlier):
+        hidden = [half[0] for half in kept[s]]
+        activ = [half[5] for half in kept[s]]
+        return pack_rows(hidden, *([half[i] for half in local] for i in (0, 1)), activ, grad, earlier)
+
+    def mix_parts(s, grad_mixed):
+        q, k, v, mixed = kept[s][2]
+        local = mix_grad(s == 0, seg_ids, q, k, v, join(grad_mixed))
+        w_query, w_key, w_value, _ = weights[s]
+        parts = []
+        for gq, gk, gv in zip(*(cut(part) for part in local)):
+            parts.append((dot_right(gq, w_query) + dot_right(gk, w_key) + dot_right(gv, w_value)).astype(bf16))
+        return parts, local
+
+    def pack_attention(s, local, grad, earlier):
+        hidden = [half[0] for half in kept[s][:2]]
+        return pack_units(s, place, hidden, *local, kept[s][2][3], grad, earlier)
+
+    def near(value):
+        return along_z(value, {0: 1, 1: 0, 2: 3, 3: 2})
+
+    def far(value):
+        return along_z(value, {2: 0, 3: 1})
+
+    grad = lax.dynamic_index_in_dim(cotangent, y, 0, keepdims=False)
+    entry = added(join(entry), branch, got)
+    outputs[2] = [entry]
+    branch = dot_plain(mlp(3, entry), weights[3][2]).astype(bf16)
+    part, local = mlp_grad(weights[3], kept[3][0], grad)
+    got = swap_x(part)
+    packed, done = pack_mlp(3, [local], [grad], part)
+    sums[3] = scattered(packed)
+    got, _, branch = tied(got, done, branch)
+    grad = finish(3, 0, grad, part, got)
+    grads[3] = [grad]
+
+    parts, local = mix_parts(2, [dot_right(grad, weights[2][3]).astype(bf16)])
+    part, got_out = tied(join(parts), swap_x(branch))
+    outputs[3] = [added(entry, branch, got_out)]
+    got = swap_x(part)
+    packed, done = pack_attention(2, local, [grad], part)
+    got, _ = tied(got, done)
+    grad = grads[2] = finish_rows(2, cut(grad), cut(part), got)
+    parts2 = add(packed[0], swap_c(packed[1]))
+
+    parts, local = zip(*(mlp_grad(weights[1], kept[1][half], grad[half]) for half in range(2)))
+    part = join(parts)
+    got = swap_x(part)
+    packed, done = pack_mlp(1, local, grad, part)
+    sums[1] = scattered(packed)
+    got, _, got_y = tied(got, done, swap_y(parts2[1]))
+    grad = grads[1] = finish_rows(1, grad, cut(part), got)
+    parts2 = add(parts2[0], got_y)
+
+    parts, local = mix_parts(0, [dot_right(half, weights[0][3]).astype(bf16) for half in grad])
+    part = join(parts)
+    got = swap_x(part)
+    packed, _ = pack_attention(0, local, grad, part)
+    parts0 = add(packed[0], swap_c(packed[1]))
+    outputs = [join(halves) for halves in outputs]
+    sent = by_index(2 * (1 - y) + x, outputs)
+    got, got_y, got_z, sent = tied(got, swap_y(parts0[1]), near(parts2[1]), sent)
+    parts0, parts2 = add(parts0[0], got_y), add(parts2[0], got_z)
+    grads[0] = finish_rows(0, grad, cut(part), got)
+    grads = [join(halves) for halves in grads]
+
+    got_z, got_far = near(parts0[1]), far(parts2)
+    gain = jnp.concatenate(gain_sums, axis=0)
+    gain = gain + swap_c(gain)
+    got_gain, sent, grad_sent = tied(swap_y(gain), sent, by_index(2 * (1 - y) + x, grads))
+    got_out, got_grad = swap_y(sent), swap_y(grad_sent)
+    gain, parts0 = gain + got_gain, add(parts0[0], got_z)
+    gain, sums[0], sums[2] = gain + near(gain), add(parts0, far(parts0)), add(parts2, got_far)
+
+    def place_rows(received):
+        placed = []
+        for rows_of, got in zip((outputs, grads), received):
+            own = by_index(2 * y + x, rows_of)
+            placed.append(jnp.stack([jnp.where(y == 0, own, got), jnp.where(y == 0, got, own)])[None])
+        return placed
+
+    results, shard, gain_own = param_shard(
+        (sums[0], sums[2]), (sums[1], sums[3]), gain, place_rows, (got_out, got_grad), y, x, z, c, d
+    )
+    return *results, shard, gain_own
+
+
 def solution(mesh):
+    if mesh.shape["section"] == 4 and mesh.shape["dp"] == 2 * DEPTH:
+        grid = jax.sharding.Mesh(mesh.devices.reshape(2, 2, DEPTH, 2), AXES)
+        function, section, dp = per_row, ("y", "x"), ("z", "c")
+    else:
+        grid, function, section, dp = mesh, per_device, "section", "dp"
     return jax.shard_map(
-        per_device,
-        mesh=mesh,
-        in_specs=(
-            P(None, "dp", None),
-            P(None, "dp", None),
-            P(None, "dp", None),
-            P("section", "dp"),
-        ),
-        out_specs=(
-            P("section", None, "dp", None),
-            P("section", None, "dp", None),
-            P("section", "dp"),
-            P("section", None),
-        ),
+        function,
+        mesh=grid,
+        in_specs=(P(None, dp, None), P(None, dp, None), P(None, dp, None), P(section, dp)),
+        out_specs=(P(section, None, dp, None), P(section, None, dp, None), P(section, dp), P(section, None)),
         check_vma=False,
     )

time: 2950 us -> 638 us (0.22)
  waiting for transfers between devices: 1650 us -> 307 us
  other arithmetic: 460 us -> 77 us
  loops' own time: 271 us -> 0 us
  matrix products: 248 us -> 46.4 us
  local copies, waits for them, and re-layouts: 191 us -> 33.4 us
  Pallas kernels: 0 us -> 86.8 us
  starting transfers between devices: 93.3 us -> 59.8 us
    unnamed x3 -> x4, waiting for transfers between devices: 604 us -> 0.07 us
    ppermute x8 -> x38, waiting for transfers between devices: 753 us -> 204 us  [the longest x34 198 us: route(): return lax.ppermute(value, AXES, pairs)]
    all_gather x1 -> x0, other arithmetic: 358 us -> none  [per_device(): gathered = lax.all_gather(shard_low, 'dp', axis=1, tiled=True)[0]]
    another operation x10 -> x0, loops' own time: 271 us -> none  [the longest x5 155 us: per_device(): lax.switch(branch_index, backward_fns, back_weights, residual, seg_ids, g...]
    dot_general x22 -> x0, matrix products: 195 us -> none  [the longest x2 43.1 us: mix_backward(): jnp.einsum('zas,aze->sze', grad_scores, query_rows[start_row_index:final_...]
    all_gather x1 -> x2, waiting for transfers between devices: 291 us -> 103 us  [the longest x1 100 us: per_row(): first = lax.all_gather(block0, GROUP)]
    pallas_call x0 -> x26, Pallas kernels: none -> 86.8 us  [the longest x2 23.3 us: mix_grad(): pl.pallas_call(partial(mix_grad_kernel, taylor), in_specs=[pl.BlockSpec(m...]
    slice x24 -> x3, local copies, waits for them, and re-layouts: 71.2 us -> 1.6 us  [the longest x1 0.9 us: source_blocks(): tail = flat_params[:, -LEFT * 128:].reshape(LEFT, 128)]
  transfers between devices with their start and end apart: 10 -> 42, of which waited for: 10 -> 24; matrix products, arithmetic and copies ran while one was open for 1% -> 17% of each run, Pallas kernels for 0% -> 11%
where the time goes in v1:
time: 638 us; the launch traced here: 627 us
  waiting for transfers between devices  307 us (48%)
  Pallas kernels  86.8 us (14%)
  other arithmetic  77 us (12%)
  starting transfers between devices  59.8 us (9%)
  matrix products  46.4 us (7%)
  local copies, waits for them, and re-layouts  33.4 us (5%)
  between operations  16.8 us (3%)
    ppermute x34, waiting for transfers between devices, route(): return lax.ppermute(value, AXES, pairs)  198 us
    all_gather x1, waiting for transfers between devices, per_row(): first = lax.all_gather(block0, GROUP)  100 us
    ppermute x34, starting transfers between devices, route(): return lax.ppermute(value, AXES, pairs)  53.1 us
    dot_general x25, matrix products, dot_plain(): return jnp.dot(first_op, second_op, preferred_element_type=jnp.float32)  27.2 us
    unnamed x336, local copies, waits for them, and re-layouts  25.9 us
    pallas_call x2, Pallas kernels, mix_grad(): pl.pallas_call(partial(mix_grad_kernel, taylor), in_specs=[pl.BlockSpec(m...  23.3 us
    pallas_call x2, Pallas kernels, pack_rows(): pl.pallas_call(partial(pack_rows_kernel, counts), in_specs=[pl.BlockSpec(...  19.7 us
    dot_general x24, matrix products, dot_right(): lax.dot_general(first_op, second_op, (((1,), (1,)), ((), ())), preferred_...  19.2 us
  transfers between devices with their start and end apart: 42, of which 24 were waited for; matrix products, arithmetic and copies ran while one was open for 17% of the time, Pallas kernels for 11%

profile of v1, /device:TPU:0, one launch (start us, length us, event | category | flops | bytes accessed | tf_op | source)
XLA Modules:
  0.0 627.4 jit_solution(6963401858820299609)
XLA Ops:
  12.6 3.8 collective-permute-done.1.right_ref
  24.4 4.0 collective-permute-start.3
  29.9 6.2 collective-permute-done.3
  36.2 17.3 %collective-permute-done.5 = bf16[2192,128]{1,0:T(8,128)(2,1)S(1)} collective-permute-done((bf16[2192,128]{1,0:T(8,128)(2,1)}, bf16[2192,128]{1,0:T(8,128)(2,1)S(1)}, u32[]{:S(2)}, u32[]{:S(2)}) %collective-permute-start.5) | collective-permute-done | bytes 561184 | tf_op jit(solution)/shard_map/ppermute | solution.py:471
  57.1 8.1 %collective-permute-start.6 = (bf16[2,1040,128]{2,1,0:T(8,128)(2,1)S(1)}, bf16[2,1040,128]{2,1,0:T(8,128)(2,1)S(1)}, u32[]{:S(2)}, u32[]{:S(2)}) collective-permute-start(bf16[2,1040,128]{2,1,0:T(8,128)(2,1)S(1)} %pad_maximum_fusion.10), channel_id=1, source_target_pairs={{0,4},{1,5},{2,6},{3,7},{8,12},{9,13},{10,14},{11,15},{16,20},{17,... | collective-permute-start | bytes 1597448 | tf_op jit(solution)/shard_map/ppermute | solution.py:471
  65.2 12.2 %collective-permute-done.6 = bf16[2,1040,128]{2,1,0:T(8,128)(2,1)S(1)} collective-permute-done((bf16[2,1040,128]{2,1,0:T(8,128)(2,1)S(1)}, bf16[2,1040,128]{2,1,0:T(8,128)(2,1)S(1)}, u32[]{:S(2)}, u32[]{:S(2)}) %collective-permute-start.6) | collective-permute-done | bytes 532512 | tf_op jit(solution)/shard_map/ppermute | solution.py:471
  78.6 100.1 %all-gather.5.cloned.1.call-done = bf16[68352,128]{1,0:T(8,128)(2,1)} async-done(((bf16[4272,128]{1,0:T(8,128)(2,1)}), bf16[68352,128]{1,0:T(8,128)(2,1)}) %all-gather.5.cloned.1.call-update) | async-done | bytes 17498128 | tf_op jit(solution)/shard_map/all_gather | solution.py:1225
  188.1 4.0 shard_map.78.refs_7_
  194.1 7.4 %shard_map.79 = (bf16[1024,1408]{1,0:T(8,128)(2,1)S(1)}, bf16[1024,1408]{1,0:T(8,128)(2,1)}, bf16[1408,1024]{1,0:T(8,128)(2,1)}, bf16[16,128]{1,0:T(8,128)(2,1)S(1)}) custom-call(bf16[16,4272,128]{2,1,0:T(8,128)(2,1)} %get-tuple-element.66.gathered_ref.refs_0_, bf16[256,1024]{1,0:T(8,128)(2,1)S(1)} %convolution_convert_fusion.4.refs_1_), custom_call_target="tpu_custom_call" | custom-call | tf_op jit(solution)/shard_map/pallas_call | solution.py:1028
  202.6 4.8 collective-permute-done.7
  214.0 4.1 collective-permute-done.8.refs_0_
  235.6 7.3 %collective-permute-done.10.refs_0_ = bf16[256,1024]{1,0:T(8,128)(2,1)} collective-permute-done((bf16[256,1024]{1,0:T(8,128)(2,1)S(1)}, bf16[256,1024]{1,0:T(8,128)(2,1)}, u32[]{:S(2)}, u32[]{:S(2)}) %collective-permute-start.10) | collective-permute-done | bytes 524320 | tf_op jit(solution)/shard_map/ppermute | solution.py:471
  248.1 4.5 shard_map.83.refs_6_
  260.2 7.4 %shard_map.84 = (bf16[1024,1408]{1,0:T(8,128)(2,1)S(1)}, bf16[1024,1408]{1,0:T(8,128)(2,1)}, bf16[1408,1024]{1,0:T(8,128)(2,1)}, bf16[16,128]{1,0:T(8,128)(2,1)S(1)}) custom-call(bf16[16,2192,128]{2,1,0:T(8,128)(2,1)} %bitcast.221, bf16[512,1024]{1,0:T(8,128)(2,1)} %pad_maximum_fusion.3.refs_1_), custom_call_target="tpu_custom_call" | custom-call | tf_op jit(solution)/shard_map/pallas_call | solution.py:1028
  269.9 8.5 %collective-permute-done.11.refs_0_ = bf16[512,1024]{1,0:T(8,128)(2,1)} collective-permute-done((bf16[512,1024]{1,0:T(8,128)(2,1)}, bf16[512,1024]{1,0:T(8,128)(2,1)}, u32[]{:S(2)}, u32[]{:S(2)}) %collective-permute-start.11) | collective-permute-done | bytes 1048608 | tf_op jit(solution)/shard_map/ppermute | solution.py:471
  292.6 10.2 %shard_map.86 = (bf16[16,2176,128]{2,1,0:T(8,128)(2,1)}, f32[8,128]{1,0:T(8,128)S(1)}) custom-call(bf16[512,1024]{1,0:T(8,128)(2,1)S(1)} %fusion.6.refs_0_, bf16[512,1408]{1,0:T(8,128)(2,1)S(1)} %get-tuple-element.167.refs_1_, bf16[512,1408]{1,0:T(8,128)(2,1)S(1)} %get-tuple-element.168.refs_2_, bf16[512,1408]{1,0:T(8,128)(2,1)} %get-tuple-element.166.refs_3_, ...), custom_call_target="tpu_custom_call" | custom-call | flops 4429185024 | bytes 16777216 | tf_op jit(solution)/shard_map/pallas_call | solution.py:1091
  305.2 5.0 convolution_convert_fusion.refs_2_
  310.2 16.8 %collective-permute-done.12.refs_0_ = bf16[512,1024]{1,0:T(8,128)(2,1)} collective-permute-done((bf16[512,1024]{1,0:T(8,128)(2,1)}, bf16[512,1024]{1,0:T(8,128)(2,1)}, u32[]{:S(2)}, u32[]{:S(2)}) %collective-permute-start.12) | collective-permute-done | bytes 1048608 | tf_op jit(solution)/shard_map/ppermute | solution.py:471
  336.2 14.1 %shard_map.88 = (bf16[512,512]{1,0:T(8,128)(2,1)S(1)}, bf16[512,512]{1,0:T(8,128)(2,1)S(1)}, bf16[512,512]{1,0:T(8,128)(2,1)S(1)}) custom-call(s32[1,512]{1,0:T(1,128)S(1)} %bitcast.218, s32[512,1]{1,0:T(8,128)S(1)} %copy-done.67, bf16[512,512]{1,0:T(8,128)(2,1)S(1)} %copy-done.56, bf16[512,512]{1,0:T(8,128)(2,1)S(1)} %copy-done.58, ...), custom_call_target="tpu_custom_call" | custom-call | flops 3221225472 | bytes 4194304 | tf_op jit(solution)/shard_map/pallas_call | solution.py:626
  368.3 7.9 %collective-permute-done.14.refs_0_ = bf16[512,1024]{1,0:T(8,128)(2,1)} collective-permute-done((bf16[512,1024]{1,0:T(8,128)(2,1)}, bf16[512,1024]{1,0:T(8,128)(2,1)}, u32[]{:S(2)}, u32[]{:S(2)}) %collective-permute-start.14) | collective-permute-done | bytes 1048608 | tf_op jit(solution)/shard_map/ppermute | solution.py:471
  398.3 9.4 %shard_map.92 = (bf16[16,2176,128]{2,1,0:T(8,128)(2,1)}, f32[8,128]{1,0:T(8,128)S(1)}) custom-call(bf16[256,1024]{1,0:T(8,128)(2,1)S(1)} %copy-done.42, bf16[256,1024]{1,0:T(8,128)(2,1)S(1)} %copy-done.44, bf16[256,1408]{1,0:T(8,128)(2,1)S(1)} %get-tuple-element.174.refs_2_, bf16[256,1408]{1,0:T(8,128)(2,1)S(1)} %get-tuple-element.172.refs_3_, ...), custom_call_target="tpu_custom_call" | custom-call | flops 4429185024 | bytes 16777216 | tf_op jit(solution)/shard_map/pallas_call | solution.py:1091
  408.4 3.9 collective-permute-done.15.refs_0_
  412.3 8.4 %collective-permute-done.17.refs_2_ = bf16[2,2048,128]{2,1,0:T(8,128)(2,1)} collective-permute-done((bf16[2,2048,128]{2,1,0:T(8,128)(2,1)}, bf16[2,2048,128]{2,1,0:T(8,128)(2,1)}, u32[]{:S(2)}, u32[]{:S(2)}) %collective-permute-start.17) | collective-permute-done | bytes 1048608 | tf_op jit(solution)/shard_map/ppermute | solution.py:471
  427.2 9.2 %shard_map.94 = (bf16[512,128]{1,0:T(8,128)(2,1)S(1)}, bf16[512,128]{1,0:T(8,128)(2,1)S(1)}, bf16[512,512]{1,0:T(8,128)(2,1)S(1)}) custom-call(s32[1,512]{1,0:T(1,128)S(1)} %bitcast.219, s32[512,1]{1,0:T(8,128)S(1)} %copy-done.68, bf16[512,128]{1,0:T(8,128)(2,1)S(1)} %pad_maximum_fusion.16.q_ref, bf16[512,128]{1,0:T(8,128)(2,1)S(1)} %copy-done.70, ...), custom_call_target="tpu_custom_call" | custom-call | flops 3221225472 | bytes 4194304 | tf_op jit(solution)/shard_map/pallas_call | solution.py:626
  456.3 4.3 select_select_fusion.2.refs_3_
  460.6 33.9 %collective-permute-done.21.refs_2_ = bf16[2048,128]{1,0:T(8,128)(2,1)} collective-permute-done((bf16[2048,128]{1,0:T(8,128)(2,1)}, bf16[2048,128]{1,0:T(8,128)(2,1)}, u32[]{:S(2)}, u32[]{:S(2)}) %collective-permute-start.21) | collective-permute-done | bytes 524320 | tf_op jit(solution)/shard_map/ppermute | solution.py:471
  506.4 23.5 %collective-permute-done.22 = bf16[2048,128]{1,0:T(8,128)(2,1)S(1)} collective-permute-done((bf16[2048,128]{1,0:T(8,128)(2,1)S(1)}, bf16[2048,128]{1,0:T(8,128)(2,1)S(1)}, u32[]{:S(2)}, u32[]{:S(2)}) %collective-permute-start.22) | collective-permute-done | bytes 524320 | tf_op jit(solution)/shard_map/ppermute | solution.py:471
  536.7 5.2 collective-permute-done.24
  544.1 20.1 %collective-permute-done.23 = bf16[2048,128]{1,0:T(8,128)(2,1)} collective-permute-done((bf16[2048,128]{1,0:T(8,128)(2,1)}, bf16[2048,128]{1,0:T(8,128)(2,1)}, u32[]{:S(2)}, u32[]{:S(2)}) %collective-permute-start.23) | collective-permute-done | bytes 524320 | tf_op jit(solution)/shard_map/ppermute | solution.py:471
  573.4 3.6 collective-permute-done.28
  579.4 7.8 %collective-permute-done.25.refs_0_ = bf16[2176,128]{1,0:T(8,128)(2,1)} collective-permute-done((bf16[2176,128]{1,0:T(8,128)(2,1)}, bf16[2176,128]{1,0:T(8,128)(2,1)}, u32[]{:S(2)}, u32[]{:S(2)}) %collective-permute-start.25) | collective-permute-done | bytes 557088 | tf_op jit(solution)/shard_map/ppermute | solution.py:471
  594.3 10.1 %collective-permute-start.35 = (f32[4,1024]{1,0:T(4,128)S(1)}, f32[4,1024]{1,0:T(4,128)S(1)}, u32[]{:S(2)}, u32[]{:S(2)}) collective-permute-start(f32[4,1024]{1,0:T(4,128)S(1)} %copy-done.132), channel_id=1, source_target_pairs={{0,4},{1,5},{2,6},{3,7},{4,0},{5,1},{6,2},{7,3},{8,12},{9,13},{10,... | collective-permute-start | bytes 49160 | tf_op jit(solution)/shard_map/ppermute | solution.py:471
  (569 shorter events, 217.1 us)
Async XLA Ops:
  7.2 171.6 %all-gather.5.cloned.1.call-start = ((), (), s32[]{:S(2)}) async-start(), calls=%async_computation.4 | async-start | bytes 18591744 | tf_op jit(solution)/shard_map/all_gather | solution.py:1225
  28.4 25.1 %collective-permute-start.5 = (bf16[2192,128]{1,0:T(8,128)(2,1)}, bf16[2192,128]{1,0:T(8,128)(2,1)S(1)}, u32[]{:S(2)}, u32[]{:S(2)}) collective-permute-start(bf16[2192,128]{1,0:T(8,128)(2,1)} %get-tuple-element.179), channel_id=1, source_target_pairs={{0,24},{1,25},{2,26},{3,27},{4,28},{5,29},{6,30},{7,31},{8,16},{9,... | collective-permute-start | bytes 1683464 | tf_op jit(solution)/shard_map/ppermute | solution.py:471
  29.4 24.2 %collective-permute-start.4 = (bf16[2192,128]{1,0:T(8,128)(2,1)}, bf16[2192,128]{1,0:T(8,128)(2,1)}, u32[]{:S(2)}, u32[]{:S(2)}) collective-permute-start(bf16[2192,128]{1,0:T(8,128)(2,1)} %get-tuple-element.178), channel_id=1, source_target_pairs={{0,16},{1,17},{2,18},{3,19},{4,20},{5,21},{6,22},{7,23},{8,24},{9,... | collective-permute-start | bytes 1683464 | tf_op jit(solution)/shard_map/ppermute | solution.py:471
  57.1 20.4 %collective-permute-start.6 = (bf16[2,1040,128]{2,1,0:T(8,128)(2,1)S(1)}, bf16[2,1040,128]{2,1,0:T(8,128)(2,1)S(1)}, u32[]{:S(2)}, u32[]{:S(2)}) collective-permute-start(bf16[2,1040,128]{2,1,0:T(8,128)(2,1)S(1)} %pad_maximum_fusion.10), channel_id=1, source_target_pairs={{0,4},{1,5},{2,6},{3,7},{8,12},{9,13},{10,14},{11,15},{16,20},{17,... | collective-permute-start | bytes 1597448 | tf_op jit(solution)/shard_map/ppermute | solution.py:471
  78.6 181.6 %all-gather.7.cloned.1.call-start = ((), (), s32[]{:S(2)}) async-start(), calls=%async_computation.5 | async-start | bytes 9539584 | tf_op jit(solution)/shard_map/all_gather | solution.py:1227
  178.8 387.5 %reduce-scatter.5.cloned.1.call-start = ((), (), s32[]{:S(2)}) async-start(), calls=%async_computation.3 | async-start | bytes 9469952 | tf_op jit(solution)/shard_map/reduce_scatter | solution.py:1161
  202.0 16.1 %collective-permute-start.8 = (bf16[256,1024]{1,0:T(8,128)(2,1)S(1)}, bf16[256,1024]{1,0:T(8,128)(2,1)}, u32[]{:S(2)}, u32[]{:S(2)}) collective-permute-start(bf16[256,1024]{1,0:T(8,128)(2,1)S(1)} %convolution_convert_fusion.3), channel_id=1, source_target_pairs={{0,8},{1,9},{2,10},{3,11},{4,12},{5,13},{6,14},{7,15},{8,0},{9,1},... | collective-permute-start | bytes 1572872 | tf_op jit(solution)/shard_map/ppermute | solution.py:471
  218.1 15.1 %collective-permute-start.9 = (bf16[256,1024]{1,0:T(8,128)(2,1)}, bf16[256,1024]{1,0:T(8,128)(2,1)S(1)}, u32[]{:S(2)}, u32[]{:S(2)}) collective-permute-start(bf16[256,1024]{1,0:T(8,128)(2,1)} %get-tuple-element.77), channel_id=1, source_target_pairs={{0,8},{1,9},{2,10},{3,11},{4,12},{5,13},{6,14},{7,15},{8,0},{9,1},... | collective-permute-start | bytes 1572872 | tf_op jit(solution)/shard_map/ppermute | solution.py:471
  227.5 15.4 %collective-permute-start.10 = (bf16[256,1024]{1,0:T(8,128)(2,1)S(1)}, bf16[256,1024]{1,0:T(8,128)(2,1)}, u32[]{:S(2)}, u32[]{:S(2)}) collective-permute-start(bf16[256,1024]{1,0:T(8,128)(2,1)S(1)} %convolution_convert_fusion.5._), channel_id=1, source_target_pairs={{0,8},{1,9},{2,10},{3,11},{4,12},{5,13},{6,14},{7,15},{8,0},{9,1},... | collective-permute-start | bytes 1572872 | tf_op jit(solution)/shard_map/ppermute | solution.py:471
  254.7 23.6 %collective-permute-start.11 = (bf16[512,1024]{1,0:T(8,128)(2,1)}, bf16[512,1024]{1,0:T(8,128)(2,1)}, u32[]{:S(2)}, u32[]{:S(2)}) collective-permute-start(bf16[512,1024]{1,0:T(8,128)(2,1)} %pad_maximum_fusion.3.refs_1_), channel_id=1, source_target_pairs={{0,8},{1,9},{2,10},{3,11},{4,12},{5,13},{6,14},{7,15},{8,0},{9,1},... | collective-permute-start | bytes 3145736 | tf_op jit(solution)/shard_map/ppermute | solution.py:471
  303.4 262.9 %reduce-scatter.3.cloned.1.call-start = ((), (), s32[]{:S(2)}) async-start(), calls=%async_computation.2 | async-start | bytes 9469952 | tf_op jit(solution)/shard_map/reduce_scatter | solution.py:1161
  303.6 23.3 %collective-permute-start.12 = (bf16[512,1024]{1,0:T(8,128)(2,1)}, bf16[512,1024]{1,0:T(8,128)(2,1)}, u32[]{:S(2)}, u32[]{:S(2)}) collective-permute-start(bf16[512,1024]{1,0:T(8,128)(2,1)} %copy-done.36), channel_id=1, source_target_pairs={{0,8},{1,9},{2,10},{3,11},{4,12},{5,13},{6,14},{7,15},{8,0},{9,1},... | collective-permute-start | bytes 3145736 | tf_op jit(solution)/shard_map/ppermute | solution.py:471
  327.0 27.8 %collective-permute-start.13 = (bf16[512,1024]{1,0:T(8,128)(2,1)}, bf16[512,1024]{1,0:T(8,128)(2,1)}, u32[]{:S(2)}, u32[]{:S(2)}) collective-permute-start(bf16[512,1024]{1,0:T(8,128)(2,1)} %get-tuple-element.92), channel_id=1, source_target_pairs={{0,8},{1,9},{2,10},{3,11},{4,12},{5,13},{6,14},{7,15},{8,0},{9,1},... | collective-permute-start | bytes 3145736 | tf_op jit(solution)/shard_map/ppermute | solution.py:471
  354.8 21.3 %collective-permute-start.14 = (bf16[512,1024]{1,0:T(8,128)(2,1)}, bf16[512,1024]{1,0:T(8,128)(2,1)}, u32[]{:S(2)}, u32[]{:S(2)}) collective-permute-start(bf16[512,1024]{1,0:T(8,128)(2,1)} %get-tuple-element.98.refs_7_), channel_id=1, source_target_pairs={{0,8},{1,9},{2,10},{3,11},{4,12},{5,13},{6,14},{7,15},{8,0},{9,1},... | collective-permute-start | bytes 3145736 | tf_op jit(solution)/shard_map/ppermute | solution.py:471
  368.3 24.6 %collective-permute-start.16 = (bf16[2,2,2048,128]{3,2,1,0:T(8,128)(2,1)}, bf16[2,2,2048,128]{3,2,1,0:T(8,128)(2,1)}, u32[]{:S(2)}, u32[]{:S(2)}) collective-permute-start(bf16[2,2,2048,128]{3,2,1,0:T(8,128)(2,1)} %slice_bitcast_fusion.1), channel_id=1, source_target_pairs={{0,1},{1,0},{2,3},{3,2},{4,5},{5,4},{6,7},{7,6},{8,9},{9,8},{10,11... | collective-permute-start | bytes 6291464 | tf_op jit(solution)/shard_map/ppermute | solution.py:471
  391.8 20.5 %collective-permute-start.15 = (bf16[512,1024]{1,0:T(8,128)(2,1)}, bf16[512,1024]{1,0:T(8,128)(2,1)}, u32[]{:S(2)}, u32[]{:S(2)}) collective-permute-start(bf16[512,1024]{1,0:T(8,128)(2,1)} %pad_maximum_fusion.5.refs_10_), channel_id=1, source_target_pairs={{0,8},{1,9},{2,10},{3,11},{4,12},{5,13},{6,14},{7,15},{8,0},{9,1},... | collective-permute-start | bytes 3145736 | tf_op jit(solution)/shard_map/ppermute | solution.py:471
  396.5 24.2 %collective-permute-start.17 = (bf16[2,2048,128]{2,1,0:T(8,128)(2,1)}, bf16[2,2048,128]{2,1,0:T(8,128)(2,1)}, u32[]{:S(2)}, u32[]{:S(2)}) collective-permute-start(bf16[2,2048,128]{2,1,0:T(8,128)(2,1)} %slice_bitcast_fusion.5), channel_id=1, source_target_pairs={{0,16},{1,17},{2,18},{3,19},{4,20},{5,21},{6,22},{7,23},{8,24},{9,... | collective-permute-start | bytes 3145736 | tf_op jit(solution)/shard_map/ppermute | solution.py:471
  444.2 50.3 %collective-permute-start.19 = (bf16[512,1024]{1,0:T(8,128)(2,1)}, bf16[512,1024]{1,0:T(8,128)(2,1)}, u32[]{:S(2)}, u32[]{:S(2)}) collective-permute-start(bf16[512,1024]{1,0:T(8,128)(2,1)} %pad_maximum_fusion.6.refs_8_), channel_id=1, source_target_pairs={{0,8},{1,9},{2,10},{3,11},{4,12},{5,13},{6,14},{7,15},{8,0},{9,1},... | collective-permute-start | bytes 3145736 | tf_op jit(solution)/shard_map/ppermute | solution.py:471
  450.0 44.6 %collective-permute-start.20 = (bf16[2,2048,128]{2,1,0:T(8,128)(2,1)}, bf16[2,2048,128]{2,1,0:T(8,128)(2,1)}, u32[]{:S(2)}, u32[]{:S(2)}) collective-permute-start(bf16[2,2048,128]{2,1,0:T(8,128)(2,1)} %slice_bitcast_fusion.3), channel_id=1, source_target_pairs={{0,16},{1,17},{2,18},{3,19},{4,20},{5,21},{6,22},{7,23},{8,24},{9,... | collective-permute-start | bytes 3145736 | tf_op jit(solution)/shard_map/ppermute | solution.py:471
  454.5 40.0 %collective-permute-start.21 = (bf16[2048,128]{1,0:T(8,128)(2,1)}, bf16[2048,128]{1,0:T(8,128)(2,1)}, u32[]{:S(2)}, u32[]{:S(2)}) collective-permute-start(bf16[2048,128]{1,0:T(8,128)(2,1)} %slice_bitcast_fusion.11), channel_id=1, source_target_pairs={{0,2},{1,3},{2,0},{3,1},{4,6},{5,7},{6,4},{7,5},{8,10},{9,11},{10,... | collective-permute-start | bytes 1572872 | tf_op jit(solution)/shard_map/ppermute | solution.py:471
  496.6 45.4 %collective-permute-start.24 = (bf16[2048,128]{1,0:T(8,128)(2,1)}, bf16[2048,128]{1,0:T(8,128)(2,1)}, u32[]{:S(2)}, u32[]{:S(2)}) collective-permute-start(bf16[2048,128]{1,0:T(8,128)(2,1)} %fusion.100), channel_id=1, source_target_pairs={{4,0},{5,1},{6,2},{7,3},{12,8},{13,9},{14,10},{15,11},{20,16},{21,... | collective-permute-start | bytes 1572872 | tf_op jit(solution)/shard_map/ppermute | solution.py:471
  500.2 29.7 %collective-permute-start.22 = (bf16[2048,128]{1,0:T(8,128)(2,1)S(1)}, bf16[2048,128]{1,0:T(8,128)(2,1)S(1)}, u32[]{:S(2)}, u32[]{:S(2)}) collective-permute-start(bf16[2048,128]{1,0:T(8,128)(2,1)S(1)} %slice_bitcast_fusion.9), channel_id=1, source_target_pairs={{0,2},{1,3},{2,0},{3,1},{4,6},{5,7},{6,4},{7,5},{8,10},{9,11},{10,... | collective-permute-start | bytes 1572872 | tf_op jit(solution)/shard_map/ppermute | solution.py:471
  505.1 29.0 %collective-permute-start.27 = (f32[4,1024]{1,0:T(4,128)S(1)}, f32[4,1024]{1,0:T(4,128)S(1)}, u32[]{:S(2)}, u32[]{:S(2)}) collective-permute-start(f32[4,1024]{1,0:T(4,128)S(1)} %fusion.135), channel_id=1, source_target_pairs={{0,16},{1,17},{2,18},{3,19},{4,20},{5,21},{6,22},{7,23},{8,24},{9,... | collective-permute-start | bytes 49160 | tf_op jit(solution)/shard_map/ppermute | solution.py:471
  530.8 33.4 %collective-permute-start.23 = (bf16[2048,128]{1,0:T(8,128)(2,1)}, bf16[2048,128]{1,0:T(8,128)(2,1)}, u32[]{:S(2)}, u32[]{:S(2)}) collective-permute-start(bf16[2048,128]{1,0:T(8,128)(2,1)} %fusion.101), channel_id=1, source_target_pairs={{4,0},{5,1},{6,2},{7,3},{12,8},{13,9},{14,10},{15,11},{20,16},{21,... | collective-permute-start | bytes 1572872 | tf_op jit(solution)/shard_map/ppermute | solution.py:471
  534.7 44.7 %collective-permute-start.29 = (bf16[512,1024]{1,0:T(8,128)(2,1)}, bf16[512,1024]{1,0:T(8,128)(2,1)}, u32[]{:S(2)}, u32[]{:S(2)}) collective-permute-start(bf16[512,1024]{1,0:T(8,128)(2,1)} %get-tuple-element.116), channel_id=1, source_target_pairs={{0,16},{1,17},{2,18},{3,19},{4,20},{5,21},{6,22},{7,23},{8,24},{9,... | collective-permute-start | bytes 3145736 | tf_op jit(solution)/shard_map/ppermute | solution.py:471
  534.7 44.7 %collective-permute-start.30 = (bf16[512,1024]{1,0:T(8,128)(2,1)}, bf16[512,1024]{1,0:T(8,128)(2,1)}, u32[]{:S(2)}, u32[]{:S(2)}) collective-permute-start(bf16[512,1024]{1,0:T(8,128)(2,1)} %get-tuple-element.117), channel_id=1, source_target_pairs={{0,16},{1,17},{2,18},{3,19},{4,20},{5,21},{6,22},{7,23},{8,24},{9,... | collective-permute-start | bytes 3145736 | tf_op jit(solution)/shard_map/ppermute | solution.py:471
  571.4 15.8 %collective-permute-start.25 = (bf16[2176,128]{1,0:T(8,128)(2,1)}, bf16[2176,128]{1,0:T(8,128)(2,1)}, u32[]{:S(2)}, u32[]{:S(2)}) collective-permute-start(bf16[2176,128]{1,0:T(8,128)(2,1)} %get-tuple-element.185), channel_id=1, source_target_pairs={{0,8},{1,9},{2,10},{3,11},{4,12},{5,13},{6,14},{7,15},{8,0},{9,1},... | collective-permute-start | bytes 1671176 | tf_op jit(solution)/shard_map/ppermute | solution.py:471
  577.7 31.7 %collective-permute-start.31 = (bf16[2176,128]{1,0:T(8,128)(2,1)}, bf16[2176,128]{1,0:T(8,128)(2,1)}, u32[]{:S(2)}, u32[]{:S(2)}) collective-permute-start(bf16[2176,128]{1,0:T(8,128)(2,1)} %get-tuple-element.184), channel_id=1, source_target_pairs={{0,16},{1,17},{2,18},{3,19},{4,20},{5,21},{6,22},{7,23},{8,24},{9,... | collective-permute-start | bytes 1671176 | tf_op jit(solution)/shard_map/ppermute | solution.py:471
  579.3 30.2 %collective-permute-start.32 = (bf16[2176,128]{1,0:T(8,128)(2,1)}, bf16[2176,128]{1,0:T(8,128)(2,1)}, u32[]{:S(2)}, u32[]{:S(2)}) collective-permute-start(bf16[2176,128]{1,0:T(8,128)(2,1)} %get-tuple-element.144), channel_id=1, source_target_pairs={{0,24},{1,25},{2,26},{3,27},{4,28},{5,29},{6,30},{7,31},{8,16},{9,... | collective-permute-start | bytes 1671176 | tf_op jit(solution)/shard_map/ppermute | solution.py:471
  592.9 16.5 %collective-permute-start.33 = (bf16[2176,128]{1,0:T(8,128)(2,1)S(1)}, bf16[2176,128]{1,0:T(8,128)(2,1)S(1)}, u32[]{:S(2)}, u32[]{:S(2)}) collective-permute-start(bf16[2176,128]{1,0:T(8,128)(2,1)S(1)} %copy-done.109), channel_id=1, source_target_pairs={{2,1}} | collective-permute-start | bytes 1671176 | tf_op jit(solution)/shard_map/ppermute | solution.py:471
  593.6 15.8 %collective-permute-start.34 = (bf16[2176,128]{1,0:T(8,128)(2,1)S(1)}, bf16[2176,128]{1,0:T(8,128)(2,1)S(1)}, u32[]{:S(2)}, u32[]{:S(2)}) collective-permute-start(bf16[2176,128]{1,0:T(8,128)(2,1)S(1)} %copy-done.107), channel_id=1, source_target_pairs={{18,1}} | collective-permute-start | bytes 1671176 | tf_op jit(solution)/shard_map/ppermute | solution.py:471
  594.3 19.6 %collective-permute-start.35 = (f32[4,1024]{1,0:T(4,128)S(1)}, f32[4,1024]{1,0:T(4,128)S(1)}, u32[]{:S(2)}, u32[]{:S(2)}) collective-permute-start(f32[4,1024]{1,0:T(4,128)S(1)} %copy-done.132), channel_id=1, source_target_pairs={{0,4},{1,5},{2,6},{3,7},{4,0},{5,1},{6,2},{7,3},{8,12},{9,13},{10,... | collective-permute-start | bytes 49160 | tf_op jit(solution)/shard_map/ppermute | solution.py:471
  (178 other events, 926.4 us)
Sparse Core Ops, SparseCore 0:
  78.7 100.0 all-gather.4
  181.6 78.5 all-gather.6
  303.5 108.2 reduce-scatter.4
  416.4 140.4 reduce-scatter.2

commit v2 on v1

--- a/solution.py
+++ b/solution.py
@@ -537,7 +537,7 @@
 
 
 def tiles(taylor, row_total):
-    step = 256 if taylor else 128
+    step = 256
     reach = row_total if taylor else 128
     return [(start, step, max(0, start - reach)) for start in range(0, row_total, step)]
 

time: 638 us -> 640 us (level)
  transfers between devices with their start and end apart: 42 -> 42, of which waited for: 24 -> 23; matrix products, arithmetic and copies ran while one was open for 17% -> 17% of each run, Pallas kernels for 11% -> 11%
where the time goes in v2:
time: 640 us; the launch traced here: 628 us
  waiting for transfers between devices  311 us (49%)
  Pallas kernels  82.3 us (13%)
  other arithmetic  77.5 us (12%)
  starting transfers between devices  61.7 us (10%)
  matrix products  46 us (7%)
  local copies, waits for them, and re-layouts  33.1 us (5%)
  between operations  16.8 us (3%)
    ppermute x34, waiting for transfers between devices, route(): return lax.ppermute(value, AXES, pairs)  202 us
    all_gather x1, waiting for transfers between devices, per_row(): first = lax.all_gather(block0, GROUP)  100 us
    ppermute x34, starting transfers between devices, route(): return lax.ppermute(value, AXES, pairs)  55 us
    dot_general x25, matrix products, dot_plain(): return jnp.dot(first_op, second_op, preferred_element_type=jnp.float32)  26.8 us
    unnamed x336, local copies, waits for them, and re-layouts  25.6 us
    pallas_call x2, Pallas kernels, pack_rows(): pl.pallas_call(partial(pack_rows_kernel, counts), in_specs=[pl.BlockSpec(...  19.7 us
    dot_general x24, matrix products, dot_right(): lax.dot_general(first_op, second_op, (((1,), (1,)), ((), ())), preferred_...  19.2 us
    pallas_call x2, Pallas kernels, mix_grad(): pl.pallas_call(partial(mix_grad_kernel, taylor), in_specs=[pl.BlockSpec(m...  18.8 us
  transfers between devices with their start and end apart: 42, of which 23 were waited for; matrix products, arithmetic and copies ran while one was open for 17% of the time, Pallas kernels for 11%

profile of v2, /device:TPU:0, one launch (start us, length us, event | category | flops | bytes accessed | tf_op | source)
XLA Modules:
  0.0 628.2 jit_solution(7246774241622946038)
XLA Ops:
  12.6 3.8 collective-permute-done.1.right_ref
  24.4 4.0 collective-permute-start.3
  29.9 6.2 collective-permute-done.3
  36.2 17.3 %collective-permute-done.5 = bf16[2192,128]{1,0:T(8,128)(2,1)S(1)} collective-permute-done((bf16[2192,128]{1,0:T(8,128)(2,1)}, bf16[2192,128]{1,0:T(8,128)(2,1)S(1)}, u32[]{:S(2)}, u32[]{:S(2)}) %collective-permute-start.5) | collective-permute-done | bytes 561184 | tf_op jit(solution)/shard_map/ppermute | solution.py:471
  57.1 8.1 %collective-permute-start.6 = (bf16[2,1040,128]{2,1,0:T(8,128)(2,1)S(1)}, bf16[2,1040,128]{2,1,0:T(8,128)(2,1)S(1)}, u32[]{:S(2)}, u32[]{:S(2)}) collective-permute-start(bf16[2,1040,128]{2,1,0:T(8,128)(2,1)S(1)} %pad_maximum_fusion.10), channel_id=1, source_target_pairs={{0,4},{1,5},{2,6},{3,7},{8,12},{9,13},{10,14},{11,15},{16,20},{17,... | collective-permute-start | bytes 1597448 | tf_op jit(solution)/shard_map/ppermute | solution.py:471
  65.2 12.2 %collective-permute-done.6 = bf16[2,1040,128]{2,1,0:T(8,128)(2,1)S(1)} collective-permute-done((bf16[2,1040,128]{2,1,0:T(8,128)(2,1)S(1)}, bf16[2,1040,128]{2,1,0:T(8,128)(2,1)S(1)}, u32[]{:S(2)}, u32[]{:S(2)}) %collective-permute-start.6) | collective-permute-done | bytes 532512 | tf_op jit(solution)/shard_map/ppermute | solution.py:471
  78.6 100.1 %all-gather.5.cloned.1.call-done = bf16[68352,128]{1,0:T(8,128)(2,1)} async-done(((bf16[4272,128]{1,0:T(8,128)(2,1)}), bf16[68352,128]{1,0:T(8,128)(2,1)}) %all-gather.5.cloned.1.call-update) | async-done | bytes 17498128 | tf_op jit(solution)/shard_map/all_gather | solution.py:1225
  188.1 4.0 shard_map.78.refs_7_
  194.1 7.4 %shard_map.79 = (bf16[1024,1408]{1,0:T(8,128)(2,1)S(1)}, bf16[1024,1408]{1,0:T(8,128)(2,1)}, bf16[1408,1024]{1,0:T(8,128)(2,1)}, bf16[16,128]{1,0:T(8,128)(2,1)S(1)}) custom-call(bf16[16,4272,128]{2,1,0:T(8,128)(2,1)} %get-tuple-element.66.gathered_ref.refs_0_, bf16[256,1024]{1,0:T(8,128)(2,1)S(1)} %convolution_convert_fusion.4.refs_1_), custom_call_target="tpu_custom_call" | custom-call | tf_op jit(solution)/shard_map/pallas_call | solution.py:1028
  202.6 4.8 collective-permute-done.7
  214.0 4.1 collective-permute-done.8.refs_0_
  235.6 7.3 %collective-permute-done.10.refs_0_ = bf16[256,1024]{1,0:T(8,128)(2,1)} collective-permute-done((bf16[256,1024]{1,0:T(8,128)(2,1)S(1)}, bf16[256,1024]{1,0:T(8,128)(2,1)}, u32[]{:S(2)}, u32[]{:S(2)}) %collective-permute-start.10) | collective-permute-done | bytes 524320 | tf_op jit(solution)/shard_map/ppermute | solution.py:471
  248.1 4.6 shard_map.83.refs_6_
  260.2 7.4 %shard_map.84 = (bf16[1024,1408]{1,0:T(8,128)(2,1)S(1)}, bf16[1024,1408]{1,0:T(8,128)(2,1)}, bf16[1408,1024]{1,0:T(8,128)(2,1)}, bf16[16,128]{1,0:T(8,128)(2,1)S(1)}) custom-call(bf16[16,2192,128]{2,1,0:T(8,128)(2,1)} %bitcast.221, bf16[512,1024]{1,0:T(8,128)(2,1)} %pad_maximum_fusion.3.refs_1_), custom_call_target="tpu_custom_call" | custom-call | tf_op jit(solution)/shard_map/pallas_call | solution.py:1028
  269.9 8.6 %collective-permute-done.11.refs_0_ = bf16[512,1024]{1,0:T(8,128)(2,1)} collective-permute-done((bf16[512,1024]{1,0:T(8,128)(2,1)}, bf16[512,1024]{1,0:T(8,128)(2,1)}, u32[]{:S(2)}, u32[]{:S(2)}) %collective-permute-start.11) | collective-permute-done | bytes 1048608 | tf_op jit(solution)/shard_map/ppermute | solution.py:471
  285.7 3.5 multiply_convert_fusion
  292.9 10.2 %shard_map.86 = (bf16[16,2176,128]{2,1,0:T(8,128)(2,1)}, f32[8,128]{1,0:T(8,128)S(1)}) custom-call(bf16[512,1024]{1,0:T(8,128)(2,1)S(1)} %fusion.6.refs_0_, bf16[512,1408]{1,0:T(8,128)(2,1)S(1)} %get-tuple-element.167.refs_1_, bf16[512,1408]{1,0:T(8,128)(2,1)S(1)} %get-tuple-element.168.refs_2_, bf16[512,1408]{1,0:T(8,128)(2,1)} %get-tuple-element.166.refs_3_, ...), custom_call_target="tpu_custom_call" | custom-call | flops 4429185024 | bytes 16777216 | tf_op jit(solution)/shard_map/pallas_call | solution.py:1091
  305.6 5.0 convolution_convert_fusion.refs_2_
  310.6 16.8 %collective-permute-done.12.refs_0_ = bf16[512,1024]{1,0:T(8,128)(2,1)} collective-permute-done((bf16[512,1024]{1,0:T(8,128)(2,1)}, bf16[512,1024]{1,0:T(8,128)(2,1)}, u32[]{:S(2)}, u32[]{:S(2)}) %collective-permute-start.12) | collective-permute-done | bytes 1048608 | tf_op jit(solution)/shard_map/ppermute | solution.py:471
  336.5 9.6 %shard_map.88 = (bf16[512,512]{1,0:T(8,128)(2,1)S(1)}, bf16[512,512]{1,0:T(8,128)(2,1)S(1)}, bf16[512,512]{1,0:T(8,128)(2,1)S(1)}) custom-call(s32[1,512]{1,0:T(1,128)S(1)} %bitcast.218, s32[512,1]{1,0:T(8,128)S(1)} %copy-done.67, bf16[512,512]{1,0:T(8,128)(2,1)S(1)} %copy-done.56, bf16[512,512]{1,0:T(8,128)(2,1)S(1)} %copy-done.58, ...), custom_call_target="tpu_custom_call" | custom-call | flops 3221225472 | bytes 4194304 | tf_op jit(solution)/shard_map/pallas_call | solution.py:626
  364.0 8.0 %collective-permute-done.14.refs_0_ = bf16[512,1024]{1,0:T(8,128)(2,1)} collective-permute-done((bf16[512,1024]{1,0:T(8,128)(2,1)}, bf16[512,1024]{1,0:T(8,128)(2,1)}, u32[]{:S(2)}, u32[]{:S(2)}) %collective-permute-start.14) | collective-permute-done | bytes 1048608 | tf_op jit(solution)/shard_map/ppermute | solution.py:471
  394.2 9.4 %shard_map.92 = (bf16[16,2176,128]{2,1,0:T(8,128)(2,1)}, f32[8,128]{1,0:T(8,128)S(1)}) custom-call(bf16[256,1024]{1,0:T(8,128)(2,1)S(1)} %copy-done.42, bf16[256,1024]{1,0:T(8,128)(2,1)S(1)} %copy-done.44, bf16[256,1408]{1,0:T(8,128)(2,1)S(1)} %get-tuple-element.174.refs_2_, bf16[256,1408]{1,0:T(8,128)(2,1)S(1)} %get-tuple-element.172.refs_3_, ...), custom_call_target="tpu_custom_call" | custom-call | flops 4429185024 | bytes 16777216 | tf_op jit(solution)/shard_map/pallas_call | solution.py:1091
  404.3 4.0 collective-permute-done.15.refs_0_
  408.2 11.1 %collective-permute-done.17.refs_2_ = bf16[2,2048,128]{2,1,0:T(8,128)(2,1)} collective-permute-done((bf16[2,2048,128]{2,1,0:T(8,128)(2,1)}, bf16[2,2048,128]{2,1,0:T(8,128)(2,1)}, u32[]{:S(2)}, u32[]{:S(2)}) %collective-permute-start.17) | collective-permute-done | bytes 1048608 | tf_op jit(solution)/shard_map/ppermute | solution.py:471
  425.7 9.2 %shard_map.94 = (bf16[512,128]{1,0:T(8,128)(2,1)S(1)}, bf16[512,128]{1,0:T(8,128)(2,1)S(1)}, bf16[512,512]{1,0:T(8,128)(2,1)S(1)}) custom-call(s32[1,512]{1,0:T(1,128)S(1)} %bitcast.219, s32[512,1]{1,0:T(8,128)S(1)} %copy-done.68, bf16[512,128]{1,0:T(8,128)(2,1)S(1)} %pad_maximum_fusion.16.q_ref, bf16[512,128]{1,0:T(8,128)(2,1)S(1)} %copy-done.70, ...), custom_call_target="tpu_custom_call" | custom-call | flops 3221225472 | bytes 4194304 | tf_op jit(solution)/shard_map/pallas_call | solution.py:626
  455.2 4.3 select_select_fusion.2.refs_3_
  459.5 36.0 %collective-permute-done.21.refs_2_ = bf16[2048,128]{1,0:T(8,128)(2,1)} collective-permute-done((bf16[2048,128]{1,0:T(8,128)(2,1)}, bf16[2048,128]{1,0:T(8,128)(2,1)}, u32[]{:S(2)}, u32[]{:S(2)}) %collective-permute-start.21) | collective-permute-done | bytes 524320 | tf_op jit(solution)/shard_map/ppermute | solution.py:471
  507.9 22.6 %collective-permute-done.22 = bf16[2048,128]{1,0:T(8,128)(2,1)S(1)} collective-permute-done((bf16[2048,128]{1,0:T(8,128)(2,1)S(1)}, bf16[2048,128]{1,0:T(8,128)(2,1)S(1)}, u32[]{:S(2)}, u32[]{:S(2)}) %collective-permute-start.22) | collective-permute-done | bytes 524320 | tf_op jit(solution)/shard_map/ppermute | solution.py:471
  540.3 25.4 %collective-permute-done.23 = bf16[2048,128]{1,0:T(8,128)(2,1)} collective-permute-done((bf16[2048,128]{1,0:T(8,128)(2,1)}, bf16[2048,128]{1,0:T(8,128)(2,1)}, u32[]{:S(2)}, u32[]{:S(2)}) %collective-permute-start.23) | collective-permute-done | bytes 524320 | tf_op jit(solution)/shard_map/ppermute | solution.py:471
  574.3 3.6 collective-permute-done.28
  580.9 7.9 %collective-permute-done.25.refs_0_ = bf16[2176,128]{1,0:T(8,128)(2,1)} collective-permute-done((bf16[2176,128]{1,0:T(8,128)(2,1)}, bf16[2176,128]{1,0:T(8,128)(2,1)}, u32[]{:S(2)}, u32[]{:S(2)}) %collective-permute-start.25) | collective-permute-done | bytes 557088 | tf_op jit(solution)/shard_map/ppermute | solution.py:471
  595.9 10.4 %collective-permute-start.35 = (f32[4,1024]{1,0:T(4,128)S(1)}, f32[4,1024]{1,0:T(4,128)S(1)}, u32[]{:S(2)}, u32[]{:S(2)}) collective-permute-start(f32[4,1024]{1,0:T(4,128)S(1)} %copy-done.132), channel_id=1, source_target_pairs={{0,4},{1,5},{2,6},{3,7},{4,0},{5,1},{6,2},{7,3},{8,12},{9,13},{10,... | collective-permute-start | bytes 49160 | tf_op jit(solution)/shard_map/ppermute | solution.py:471
  (569 shorter events, 214.4 us)
Async XLA Ops:
  7.2 171.6 %all-gather.5.cloned.1.call-start = ((), (), s32[]{:S(2)}) async-start(), calls=%async_computation.4 | async-start | bytes 18591744 | tf_op jit(solution)/shard_map/all_gather | solution.py:1225
  28.4 25.1 %collective-permute-start.5 = (bf16[2192,128]{1,0:T(8,128)(2,1)}, bf16[2192,128]{1,0:T(8,128)(2,1)S(1)}, u32[]{:S(2)}, u32[]{:S(2)}) collective-permute-start(bf16[2192,128]{1,0:T(8,128)(2,1)} %get-tuple-element.179), channel_id=1, source_target_pairs={{0,24},{1,25},{2,26},{3,27},{4,28},{5,29},{6,30},{7,31},{8,16},{9,... | collective-permute-start | bytes 1683464 | tf_op jit(solution)/shard_map/ppermute | solution.py:471
  29.4 24.2 %collective-permute-start.4 = (bf16[2192,128]{1,0:T(8,128)(2,1)}, bf16[2192,128]{1,0:T(8,128)(2,1)}, u32[]{:S(2)}, u32[]{:S(2)}) collective-permute-start(bf16[2192,128]{1,0:T(8,128)(2,1)} %get-tuple-element.178), channel_id=1, source_target_pairs={{0,16},{1,17},{2,18},{3,19},{4,20},{5,21},{6,22},{7,23},{8,24},{9,... | collective-permute-start | bytes 1683464 | tf_op jit(solution)/shard_map/ppermute | solution.py:471
  57.1 20.4 %collective-permute-start.6 = (bf16[2,1040,128]{2,1,0:T(8,128)(2,1)S(1)}, bf16[2,1040,128]{2,1,0:T(8,128)(2,1)S(1)}, u32[]{:S(2)}, u32[]{:S(2)}) collective-permute-start(bf16[2,1040,128]{2,1,0:T(8,128)(2,1)S(1)} %pad_maximum_fusion.10), channel_id=1, source_target_pairs={{0,4},{1,5},{2,6},{3,7},{8,12},{9,13},{10,14},{11,15},{16,20},{17,... | collective-permute-start | bytes 1597448 | tf_op jit(solution)/shard_map/ppermute | solution.py:471
  78.6 181.6 %all-gather.7.cloned.1.call-start = ((), (), s32[]{:S(2)}) async-start(), calls=%async_computation.5 | async-start | bytes 9539584 | tf_op jit(solution)/shard_map/all_gather | solution.py:1227
  178.8 389.1 %reduce-scatter.5.cloned.1.call-start = ((), (), s32[]{:S(2)}) async-start(), calls=%async_computation.3 | async-start | bytes 9469952 | tf_op jit(solution)/shard_map/reduce_scatter | solution.py:1161
  202.0 16.1 %collective-permute-start.8 = (bf16[256,1024]{1,0:T(8,128)(2,1)S(1)}, bf16[256,1024]{1,0:T(8,128)(2,1)}, u32[]{:S(2)}, u32[]{:S(2)}) collective-permute-start(bf16[256,1024]{1,0:T(8,128)(2,1)S(1)} %convolution_convert_fusion.3), channel_id=1, source_target_pairs={{0,8},{1,9},{2,10},{3,11},{4,12},{5,13},{6,14},{7,15},{8,0},{9,1},... | collective-permute-start | bytes 1572872 | tf_op jit(solution)/shard_map/ppermute | solution.py:471
  218.1 15.1 %collective-permute-start.9 = (bf16[256,1024]{1,0:T(8,128)(2,1)}, bf16[256,1024]{1,0:T(8,128)(2,1)S(1)}, u32[]{:S(2)}, u32[]{:S(2)}) collective-permute-start(bf16[256,1024]{1,0:T(8,128)(2,1)} %get-tuple-element.77), channel_id=1, source_target_pairs={{0,8},{1,9},{2,10},{3,11},{4,12},{5,13},{6,14},{7,15},{8,0},{9,1},... | collective-permute-start | bytes 1572872 | tf_op jit(solution)/shard_map/ppermute | solution.py:471
  227.5 15.4 %collective-permute-start.10 = (bf16[256,1024]{1,0:T(8,128)(2,1)S(1)}, bf16[256,1024]{1,0:T(8,128)(2,1)}, u32[]{:S(2)}, u32[]{:S(2)}) collective-permute-start(bf16[256,1024]{1,0:T(8,128)(2,1)S(1)} %convolution_convert_fusion.5._), channel_id=1, source_target_pairs={{0,8},{1,9},{2,10},{3,11},{4,12},{5,13},{6,14},{7,15},{8,0},{9,1},... | collective-permute-start | bytes 1572872 | tf_op jit(solution)/shard_map/ppermute | solution.py:471
  254.8 23.6 %collective-permute-start.11 = (bf16[512,1024]{1,0:T(8,128)(2,1)}, bf16[512,1024]{1,0:T(8,128)(2,1)}, u32[]{:S(2)}, u32[]{:S(2)}) collective-permute-start(bf16[512,1024]{1,0:T(8,128)(2,1)} %pad_maximum_fusion.3.refs_1_), channel_id=1, source_target_pairs={{0,8},{1,9},{2,10},{3,11},{4,12},{5,13},{6,14},{7,15},{8,0},{9,1},... | collective-permute-start | bytes 3145736 | tf_op jit(solution)/shard_map/ppermute | solution.py:471
  303.8 264.1 %reduce-scatter.3.cloned.1.call-start = ((), (), s32[]{:S(2)}) async-start(), calls=%async_computation.2 | async-start | bytes 9469952 | tf_op jit(solution)/shard_map/reduce_scatter | solution.py:1161
  304.0 23.3 %collective-permute-start.12 = (bf16[512,1024]{1,0:T(8,128)(2,1)}, bf16[512,1024]{1,0:T(8,128)(2,1)}, u32[]{:S(2)}, u32[]{:S(2)}) collective-permute-start(bf16[512,1024]{1,0:T(8,128)(2,1)} %copy-done.36), channel_id=1, source_target_pairs={{0,8},{1,9},{2,10},{3,11},{4,12},{5,13},{6,14},{7,15},{8,0},{9,1},... | collective-permute-start | bytes 3145736 | tf_op jit(solution)/shard_map/ppermute | solution.py:471
  327.4 23.3 %collective-permute-start.13 = (bf16[512,1024]{1,0:T(8,128)(2,1)}, bf16[512,1024]{1,0:T(8,128)(2,1)}, u32[]{:S(2)}, u32[]{:S(2)}) collective-permute-start(bf16[512,1024]{1,0:T(8,128)(2,1)} %get-tuple-element.92), channel_id=1, source_target_pairs={{0,8},{1,9},{2,10},{3,11},{4,12},{5,13},{6,14},{7,15},{8,0},{9,1},... | collective-permute-start | bytes 3145736 | tf_op jit(solution)/shard_map/ppermute | solution.py:471
  350.6 21.3 %collective-permute-start.14 = (bf16[512,1024]{1,0:T(8,128)(2,1)}, bf16[512,1024]{1,0:T(8,128)(2,1)}, u32[]{:S(2)}, u32[]{:S(2)}) collective-permute-start(bf16[512,1024]{1,0:T(8,128)(2,1)} %get-tuple-element.98.refs_7_), channel_id=1, source_target_pairs={{0,8},{1,9},{2,10},{3,11},{4,12},{5,13},{6,14},{7,15},{8,0},{9,1},... | collective-permute-start | bytes 3145736 | tf_op jit(solution)/shard_map/ppermute | solution.py:471
  364.0 25.0 %collective-permute-start.16 = (bf16[2,2,2048,128]{3,2,1,0:T(8,128)(2,1)}, bf16[2,2,2048,128]{3,2,1,0:T(8,128)(2,1)}, u32[]{:S(2)}, u32[]{:S(2)}) collective-permute-start(bf16[2,2,2048,128]{3,2,1,0:T(8,128)(2,1)} %slice_bitcast_fusion.1), channel_id=1, source_target_pairs={{0,1},{1,0},{2,3},{3,2},{4,5},{5,4},{6,7},{7,6},{8,9},{9,8},{10,11... | collective-permute-start | bytes 6291464 | tf_op jit(solution)/shard_map/ppermute | solution.py:471
  387.8 20.4 %collective-permute-start.15 = (bf16[512,1024]{1,0:T(8,128)(2,1)}, bf16[512,1024]{1,0:T(8,128)(2,1)}, u32[]{:S(2)}, u32[]{:S(2)}) collective-permute-start(bf16[512,1024]{1,0:T(8,128)(2,1)} %pad_maximum_fusion.5.refs_10_), channel_id=1, source_target_pairs={{0,8},{1,9},{2,10},{3,11},{4,12},{5,13},{6,14},{7,15},{8,0},{9,1},... | collective-permute-start | bytes 3145736 | tf_op jit(solution)/shard_map/ppermute | solution.py:471
  392.7 26.6 %collective-permute-start.17 = (bf16[2,2048,128]{2,1,0:T(8,128)(2,1)}, bf16[2,2048,128]{2,1,0:T(8,128)(2,1)}, u32[]{:S(2)}, u32[]{:S(2)}) collective-permute-start(bf16[2,2048,128]{2,1,0:T(8,128)(2,1)} %slice_bitcast_fusion.5), channel_id=1, source_target_pairs={{0,16},{1,17},{2,18},{3,19},{4,20},{5,21},{6,22},{7,23},{8,24},{9,... | collective-permute-start | bytes 3145736 | tf_op jit(solution)/shard_map/ppermute | solution.py:471
  443.1 52.4 %collective-permute-start.19 = (bf16[512,1024]{1,0:T(8,128)(2,1)}, bf16[512,1024]{1,0:T(8,128)(2,1)}, u32[]{:S(2)}, u32[]{:S(2)}) collective-permute-start(bf16[512,1024]{1,0:T(8,128)(2,1)} %pad_maximum_fusion.6.refs_8_), channel_id=1, source_target_pairs={{0,8},{1,9},{2,10},{3,11},{4,12},{5,13},{6,14},{7,15},{8,0},{9,1},... | collective-permute-start | bytes 3145736 | tf_op jit(solution)/shard_map/ppermute | solution.py:471
  448.9 46.7 %collective-permute-start.20 = (bf16[2,2048,128]{2,1,0:T(8,128)(2,1)}, bf16[2,2048,128]{2,1,0:T(8,128)(2,1)}, u32[]{:S(2)}, u32[]{:S(2)}) collective-permute-start(bf16[2,2048,128]{2,1,0:T(8,128)(2,1)} %slice_bitcast_fusion.3), channel_id=1, source_target_pairs={{0,16},{1,17},{2,18},{3,19},{4,20},{5,21},{6,22},{7,23},{8,24},{9,... | collective-permute-start | bytes 3145736 | tf_op jit(solution)/shard_map/ppermute | solution.py:471
  453.5 42.0 %collective-permute-start.21 = (bf16[2048,128]{1,0:T(8,128)(2,1)}, bf16[2048,128]{1,0:T(8,128)(2,1)}, u32[]{:S(2)}, u32[]{:S(2)}) collective-permute-start(bf16[2048,128]{1,0:T(8,128)(2,1)} %slice_bitcast_fusion.11), channel_id=1, source_target_pairs={{0,2},{1,3},{2,0},{3,1},{4,6},{5,7},{6,4},{7,5},{8,10},{9,11},{10,... | collective-permute-start | bytes 1572872 | tf_op jit(solution)/shard_map/ppermute | solution.py:471
  497.6 40.6 %collective-permute-start.24 = (bf16[2048,128]{1,0:T(8,128)(2,1)}, bf16[2048,128]{1,0:T(8,128)(2,1)}, u32[]{:S(2)}, u32[]{:S(2)}) collective-permute-start(bf16[2048,128]{1,0:T(8,128)(2,1)} %fusion.100), channel_id=1, source_target_pairs={{4,0},{5,1},{6,2},{7,3},{12,8},{13,9},{14,10},{15,11},{20,16},{21,... | collective-permute-start | bytes 1572872 | tf_op jit(solution)/shard_map/ppermute | solution.py:471
  501.3 29.2 %collective-permute-start.22 = (bf16[2048,128]{1,0:T(8,128)(2,1)S(1)}, bf16[2048,128]{1,0:T(8,128)(2,1)S(1)}, u32[]{:S(2)}, u32[]{:S(2)}) collective-permute-start(bf16[2048,128]{1,0:T(8,128)(2,1)S(1)} %slice_bitcast_fusion.9), channel_id=1, source_target_pairs={{0,2},{1,3},{2,0},{3,1},{4,6},{5,7},{6,4},{7,5},{8,10},{9,11},{10,... | collective-permute-start | bytes 1572872 | tf_op jit(solution)/shard_map/ppermute | solution.py:471
  506.3 28.4 %collective-permute-start.27 = (f32[4,1024]{1,0:T(4,128)S(1)}, f32[4,1024]{1,0:T(4,128)S(1)}, u32[]{:S(2)}, u32[]{:S(2)}) collective-permute-start(f32[4,1024]{1,0:T(4,128)S(1)} %fusion.135), channel_id=1, source_target_pairs={{0,16},{1,17},{2,18},{3,19},{4,20},{5,21},{6,22},{7,23},{8,24},{9,... | collective-permute-start | bytes 49160 | tf_op jit(solution)/shard_map/ppermute | solution.py:471
  531.4 34.3 %collective-permute-start.23 = (bf16[2048,128]{1,0:T(8,128)(2,1)}, bf16[2048,128]{1,0:T(8,128)(2,1)}, u32[]{:S(2)}, u32[]{:S(2)}) collective-permute-start(bf16[2048,128]{1,0:T(8,128)(2,1)} %fusion.101), channel_id=1, source_target_pairs={{4,0},{5,1},{6,2},{7,3},{12,8},{13,9},{14,10},{15,11},{20,16},{21,... | collective-permute-start | bytes 1572872 | tf_op jit(solution)/shard_map/ppermute | solution.py:471
  535.3 45.6 %collective-permute-start.29 = (bf16[512,1024]{1,0:T(8,128)(2,1)}, bf16[512,1024]{1,0:T(8,128)(2,1)}, u32[]{:S(2)}, u32[]{:S(2)}) collective-permute-start(bf16[512,1024]{1,0:T(8,128)(2,1)} %get-tuple-element.116), channel_id=1, source_target_pairs={{0,16},{1,17},{2,18},{3,19},{4,20},{5,21},{6,22},{7,23},{8,24},{9,... | collective-permute-start | bytes 3145736 | tf_op jit(solution)/shard_map/ppermute | solution.py:471
  538.1 42.8 %collective-permute-start.30 = (bf16[512,1024]{1,0:T(8,128)(2,1)}, bf16[512,1024]{1,0:T(8,128)(2,1)}, u32[]{:S(2)}, u32[]{:S(2)}) collective-permute-start(bf16[512,1024]{1,0:T(8,128)(2,1)} %get-tuple-element.117), channel_id=1, source_target_pairs={{0,16},{1,17},{2,18},{3,19},{4,20},{5,21},{6,22},{7,23},{8,24},{9,... | collective-permute-start | bytes 3145736 | tf_op jit(solution)/shard_map/ppermute | solution.py:471
  572.9 15.9 %collective-permute-start.25 = (bf16[2176,128]{1,0:T(8,128)(2,1)}, bf16[2176,128]{1,0:T(8,128)(2,1)}, u32[]{:S(2)}, u32[]{:S(2)}) collective-permute-start(bf16[2176,128]{1,0:T(8,128)(2,1)} %get-tuple-element.185), channel_id=1, source_target_pairs={{0,8},{1,9},{2,10},{3,11},{4,12},{5,13},{6,14},{7,15},{8,0},{9,1},... | collective-permute-start | bytes 1671176 | tf_op jit(solution)/shard_map/ppermute | solution.py:471
  578.6 31.7 %collective-permute-start.31 = (bf16[2176,128]{1,0:T(8,128)(2,1)}, bf16[2176,128]{1,0:T(8,128)(2,1)}, u32[]{:S(2)}, u32[]{:S(2)}) collective-permute-start(bf16[2176,128]{1,0:T(8,128)(2,1)} %get-tuple-element.184), channel_id=1, source_target_pairs={{0,16},{1,17},{2,18},{3,19},{4,20},{5,21},{6,22},{7,23},{8,24},{9,... | collective-permute-start | bytes 1671176 | tf_op jit(solution)/shard_map/ppermute | solution.py:471
  579.4 30.8 %collective-permute-start.32 = (bf16[2176,128]{1,0:T(8,128)(2,1)}, bf16[2176,128]{1,0:T(8,128)(2,1)}, u32[]{:S(2)}, u32[]{:S(2)}) collective-permute-start(bf16[2176,128]{1,0:T(8,128)(2,1)} %get-tuple-element.144), channel_id=1, source_target_pairs={{0,24},{1,25},{2,26},{3,27},{4,28},{5,29},{6,30},{7,31},{8,16},{9,... | collective-permute-start | bytes 1671176 | tf_op jit(solution)/shard_map/ppermute | solution.py:471
  594.5 15.8 %collective-permute-start.33 = (bf16[2176,128]{1,0:T(8,128)(2,1)S(1)}, bf16[2176,128]{1,0:T(8,128)(2,1)S(1)}, u32[]{:S(2)}, u32[]{:S(2)}) collective-permute-start(bf16[2176,128]{1,0:T(8,128)(2,1)S(1)} %copy-done.109), channel_id=1, source_target_pairs={{2,1}} | collective-permute-start | bytes 1671176 | tf_op jit(solution)/shard_map/ppermute | solution.py:471
  595.2 15.0 %collective-permute-start.34 = (bf16[2176,128]{1,0:T(8,128)(2,1)S(1)}, bf16[2176,128]{1,0:T(8,128)(2,1)S(1)}, u32[]{:S(2)}, u32[]{:S(2)}) collective-permute-start(bf16[2176,128]{1,0:T(8,128)(2,1)S(1)} %copy-done.107), channel_id=1, source_target_pairs={{18,1}} | collective-permute-start | bytes 1671176 | tf_op jit(solution)/shard_map/ppermute | solution.py:471
  595.9 18.8 %collective-permute-start.35 = (f32[4,1024]{1,0:T(4,128)S(1)}, f32[4,1024]{1,0:T(4,128)S(1)}, u32[]{:S(2)}, u32[]{:S(2)}) collective-permute-start(f32[4,1024]{1,0:T(4,128)S(1)} %copy-done.132), channel_id=1, source_target_pairs={{0,4},{1,5},{2,6},{3,7},{4,0},{5,1},{6,2},{7,3},{8,12},{9,13},{10,... | collective-permute-start | bytes 49160 | tf_op jit(solution)/shard_map/ppermute | solution.py:471
  (178 other events, 926.6 us)
Sparse Core Ops, SparseCore 0:
  78.7 100.0 all-gather.4
  181.6 78.5 all-gather.6
  303.9 111.2 reduce-scatter.4
  419.7 141.4 reduce-scatter.2
